TPU v7x, 128 devices: a whole 4x4x4 slice. The times are simulated.
128 devices in a mesh: frame: 8 (over y, z_lo), patch: 16 (over z_hi, x, core).
Axes of the slice: x: 4, y: 4, z: 4 (z_hi: 2, z_lo: 2; z = z_hi * 2 + z_lo), core: 2. Of those that a mesh axis runs over, the one named last changes fastest.
Arguments:
- tokens: bfloat16 [32, 2048, 1152], P('frame', 'patch'), may hold values from -6 to 6
- w_qkv_s: bfloat16 [1152, 3456], replicated, may hold values from -0.70710678 to 0.70710678
- w_out_s: bfloat16 [1152, 1152], replicated, may hold values from -0.1875 to 0.1875
- mod_s: float32 [3, 1152], replicated, may hold values from -2 to 2, as said below
- w_qkv_t: bfloat16 [1152, 3456], replicated, may hold values from -0.70710678 to 0.70710678
- w_out_t: bfloat16 [1152, 1152], replicated, may hold values from -0.1875 to 0.1875
- mod_t: float32 [3, 1152], replicated, may hold values from -2 to 2, as said below
Outputs:
- blocked: bfloat16 [32, 2048, 1152], P('frame', 'patch')
Inputs may be any that keep to these rules, and one draw needn't show every extreme that they name: `mod_s`: row 1 lies in -0.5 to 0.5, row 2 in 0.5 to 1.5. `mod_t`: row 1 lies in -0.5 to 0.5, row 2 in 0.5 to 1.5.
All inputs are finite; a program needn't handle non-finite values.
Results may differ from a plain program's by a relative error of at most 0.017.
Values may be sent and summed in bfloat16 or wider, within the bound.
A program may use at most 128 MiB of HBM per device.

v0:
```python
import jax
import jax.numpy as jnp
from jax import lax
from jax.sharding import PartitionSpec as P

HEADS = 16
HD = 72


def layer_norm(values):
    mean = jnp.mean(values, axis=-1, keepdims=True)
    centered = values - mean
    var = jnp.mean(centered * centered, axis=-1, keepdims=True)
    return centered * lax.rsqrt(var + 1e-06)


def project_qkv(values, weight, mod_rows):
    frames, patches, width = values.shape
    normed = layer_norm(values.astype(jnp.float32)) * (1.0 + mod_rows[1]) + mod_rows[0]
    normed = normed.astype(jnp.bfloat16).reshape(frames * patches, width)
    mixed = jnp.dot(normed, weight, preferred_element_type=jnp.float32).astype(jnp.bfloat16)
    return mixed.reshape(frames, patches, 3, HEADS, HD)


def spatial_frame(qkv_frame):
    scores = jnp.einsum(
        "qhd,khd->hqk", qkv_frame[:, 0], qkv_frame[:, 1], preferred_element_type=jnp.float32
    ) * HD ** (-0.5)
    top = jnp.max(scores, axis=-1, keepdims=True)
    expo = jnp.exp(scores - top)
    probs = (expo / jnp.sum(expo, axis=-1, keepdims=True)).astype(jnp.bfloat16)
    return jnp.einsum(
        "hqk,khd->qhd", probs, qkv_frame[:, 2], preferred_element_type=jnp.float32
    ).astype(jnp.bfloat16)


def temporal_attend(qkv):
    scores = jnp.einsum(
        "fphd,gphd->phfg", qkv[:, :, 0], qkv[:, :, 1], preferred_element_type=jnp.float32
    ) * HD ** (-0.5)
    top = jnp.max(scores, axis=-1, keepdims=True)
    expo = jnp.exp(scores - top)
    probs = (expo / jnp.sum(expo, axis=-1, keepdims=True)).astype(jnp.bfloat16)
    return jnp.einsum(
        "phfg,gphd->fphd", probs, qkv[:, :, 2], preferred_element_type=jnp.float32
    ).astype(jnp.bfloat16)


def finish(values, attended, weight, mod_rows):
    frames, patches, width = values.shape
    proj = jnp.dot(
        attended.reshape(frames * patches, width), weight, preferred_element_type=jnp.float32
    )
    proj = proj.reshape(frames, patches, width)
    return (values.astype(jnp.float32) + mod_rows[2] * proj).astype(jnp.bfloat16)


def spatial_items(block):
    attended = lax.map(spatial_frame, block)
    return lax.all_to_all(attended, "patch", split_axis=1, concat_axis=2, tiled=True)


def temporal_items(block):
    attended = temporal_attend(block)
    return lax.all_to_all(attended, "frame", split_axis=0, concat_axis=2, tiled=True)


def shards(tokens, w_qkv_s, w_out_s, mod_s, w_qkv_t, w_out_t, mod_t):
    qkv = project_qkv(tokens, w_qkv_s, mod_s)
    attended = spatial_items(lax.all_to_all(qkv, "patch", split_axis=3, concat_axis=1, tiled=True))
    middle = finish(tokens, attended, w_out_s, mod_s)
    qkv_time = project_qkv(middle, w_qkv_t, mod_t)
    attended_time = temporal_items(
        lax.all_to_all(qkv_time, "frame", split_axis=3, concat_axis=0, tiled=True)
    )
    blocked = finish(middle, attended_time, w_out_t, mod_t)
    return blocked


def solution(mesh):
    return jax.shard_map(
        shards,
        mesh=mesh,
        in_specs=(P("frame", "patch", None), P(), P(), P(), P(), P(), P()),
        out_specs=P("frame", "patch", None),
        check_vma=False,
    )
```

profile of v0, /device:TPU:32, one launch (start us, length us, event | category | flops | bytes accessed | tf_op | source)
XLA Modules:
  0.0 392.8 jit_solution(8907045617904933162)
XLA Ops:
  5.3 9.7 %convolution_convert_fusion.1 = bf16[512,3456]{1,0:T(8,128)(2,1)} fusion(bf16[512,1152]{1,0:T(8,128)(2,1)S(1)} %bitcast.90, bf16[1152,3456]{1,0:T(8,128)(2,1)} %param.10), kind=kOutput, calls=%fused_computation.16 | convolution fusion | flops 4078632960 | bytes 12681216 | tf_op jit(solution)/shard_map/dot_general | solution.py:21
  15.0 13.7 %reshape.104 = bf16[4,128,3,16,72]{4,3,2,1,0:T(8,128)(2,1)} reshape(bf16[512,3456]{1,0:T(8,128)(2,1)} %convolution_convert_fusion.1) | data formatting | bytes 7077888 | tf_op jit(solution)/shard_map/reshape | solution.py:22
  28.7 8.3 %copy.62 = bf16[4,128,3,16,72]{1,0,4,2,3:T(4,128)(2,1)} copy(bf16[4,128,3,16,72]{4,3,2,1,0:T(8,128)(2,1)} %reshape.104) | data formatting | bytes 7077888 | tf_op jit(solution)/shard_map/reshape | solution.py:22
  43.9 47.5 %all-to-all-done = bf16[4,128,3,16,72]{1,0,4,2,3:T(4,128)(2,1)} async-done(((bf16[4,128,3,16,72]{1,0,4,2,3:T(4,128)(2,1)}), bf16[4,128,3,16,72]{1,0,4,2,3:T(4,128)(2,1)}, u32[]{:S(2)}, u32[]{:S(2)}) %all-to-all-start) | async-done | bytes 3538976 | tf_op jit(solution)/shard_map/all_to_all | solution.py:70
  103.1 104.8 %while.10 = (s32[]{:T(128)}, bf16[4,2048,1,72]{1,3,2,0:T(8,128)(2,1)}, bf16[4,2048,3,1,72]{1,4,3,2,0:T(8,128)(2,1)}, s32[]{:T(128)}) while((s32[]{:T(128)}, bf16[4,2048,1,72]{1,3,2,0:T(8,128)(2,1)}, bf16[4,2048,3,1,72]{1,4,3,2,0:T(8,128)(2,1)}, s32[]{:T(128)}) %tuple.35), condition=%wide.region_5.6_spmd, body=%wide.region_2.5_spmd.sunk | while | flops 1245851648 | bytes 53322296 | solution.py:59
  104.3 8.1 %multiply_reduce_fusion.3 = (f32[2048]{0:T(1024)S(1)}, f32[2048,2048]{0,1:T(8,128)}) fusion(bf16[2048,3,1,72]{0,3,2,1:T(8,128)(2,1)S(1)} %dynamic-slice_bitcast_fusion.2), kind=kOutput, calls=%fused_computation.2.clone.1 | convolution fusion | flops 612366336 | bytes 17375232 | tf_op jit(solution)/shard_map/while/body/eval_jaxpr/qhd,khd->hqk/dot_general | solution.py:26
  112.4 8.6 %fusion.41 = f32[2048]{0:T(1024)S(1)} fusion(f32[2048,2048]{0,1:T(8,128)} %get-tuple-element.77, f32[2048]{0:T(1024)S(1)} %get-tuple-element.78), kind=kLoop, calls=%fused_computation.3.clone.1 | loop fusion | flops 12580864 | bytes 16793600 | tf_op jit(solution)/shard_map/while/body/eval_jaxpr/reduce_sum | solution.py:31
  121.0 8.3 %fusion.42 = bf16[4,2048,1,72]{1,3,2,0:T(8,128)(2,1)} fusion(bf16[4,2048,1,72]{1,3,2,0:T(8,128)(2,1)} %get-tuple-element.84, s32[]{:T(128)} %get-tuple-element.83, f32[2048,2048]{0,1:T(8,128)} %get-tuple-element.77, f32[2048]{0:T(1024)S(1)} %fusion.41, f32[2048]{0:T(1024)S(1)} %get-tuple-element.78, ...), kind=kOutput, calls=%fused_computation.7.clone.1 | convolution fusion | flops 620904448 | bytes 17383936 | tf_op jit(solution)/shard_map/while/body/eval_jaxpr/hqk,khd->qhd/dot_general | solution.py:32
  138.6 8.6 %fusion.41 = f32[2048]{0:T(1024)S(1)} fusion(f32[2048,2048]{0,1:T(8,128)} %get-tuple-element.77, f32[2048]{0:T(1024)S(1)} %get-tuple-element.78), kind=kLoop, calls=%fused_computation.3.clone.1 | loop fusion | flops 12580864 | bytes 16793600 | tf_op jit(solution)/shard_map/while/body/eval_jaxpr/reduce_sum | solution.py:31
  147.2 8.3 %fusion.42 = bf16[4,2048,1,72]{1,3,2,0:T(8,128)(2,1)} fusion(bf16[4,2048,1,72]{1,3,2,0:T(8,128)(2,1)} %get-tuple-element.84, s32[]{:T(128)} %get-tuple-element.83, f32[2048,2048]{0,1:T(8,128)} %get-tuple-element.77, f32[2048]{0:T(1024)S(1)} %fusion.41, f32[2048]{0:T(1024)S(1)} %get-tuple-element.78, ...), kind=kOutput, calls=%fused_computation.7.clone.1 | convolution fusion | flops 620904448 | bytes 17383936 | tf_op jit(solution)/shard_map/while/body/eval_jaxpr/hqk,khd->qhd/dot_general | solution.py:32
  156.7 8.1 %multiply_reduce_fusion.3 = (f32[2048]{0:T(1024)S(1)}, f32[2048,2048]{0,1:T(8,128)}) fusion(bf16[2048,3,1,72]{0,3,2,1:T(8,128)(2,1)S(1)} %dynamic-slice_bitcast_fusion.2), kind=kOutput, calls=%fused_computation.2.clone.1 | convolution fusion | flops 612366336 | bytes 17375232 | tf_op jit(solution)/shard_map/while/body/eval_jaxpr/qhd,khd->hqk/dot_general | solution.py:26
  164.8 8.6 %fusion.41 = f32[2048]{0:T(1024)S(1)} fusion(f32[2048,2048]{0,1:T(8,128)} %get-tuple-element.77, f32[2048]{0:T(1024)S(1)} %get-tuple-element.78), kind=kLoop, calls=%fused_computation.3.clone.1 | loop fusion | flops 12580864 | bytes 16793600 | tf_op jit(solution)/shard_map/while/body/eval_jaxpr/reduce_sum | solution.py:31
  173.4 8.3 %fusion.42 = bf16[4,2048,1,72]{1,3,2,0:T(8,128)(2,1)} fusion(bf16[4,2048,1,72]{1,3,2,0:T(8,128)(2,1)} %get-tuple-element.84, s32[]{:T(128)} %get-tuple-element.83, f32[2048,2048]{0,1:T(8,128)} %get-tuple-element.77, f32[2048]{0:T(1024)S(1)} %fusion.41, f32[2048]{0:T(1024)S(1)} %get-tuple-element.78, ...), kind=kOutput, calls=%fused_computation.7.clone.1 | convolution fusion | flops 620904448 | bytes 17383936 | tf_op jit(solution)/shard_map/while/body/eval_jaxpr/hqk,khd->qhd/dot_general | solution.py:32
  182.9 8.1 %multiply_reduce_fusion.3 = (f32[2048]{0:T(1024)S(1)}, f32[2048,2048]{0,1:T(8,128)}) fusion(bf16[2048,3,1,72]{0,3,2,1:T(8,128)(2,1)S(1)} %dynamic-slice_bitcast_fusion.2), kind=kOutput, calls=%fused_computation.2.clone.1 | convolution fusion | flops 612366336 | bytes 17375232 | tf_op jit(solution)/shard_map/while/body/eval_jaxpr/qhd,khd->hqk/dot_general | solution.py:26
  191.0 8.6 %fusion.41 = f32[2048]{0:T(1024)S(1)} fusion(f32[2048,2048]{0,1:T(8,128)} %get-tuple-element.77, f32[2048]{0:T(1024)S(1)} %get-tuple-element.78), kind=kLoop, calls=%fused_computation.3.clone.1 | loop fusion | flops 12580864 | bytes 16793600 | tf_op jit(solution)/shard_map/while/body/eval_jaxpr/reduce_sum | solution.py:31
  199.6 8.3 %fusion.42 = bf16[4,2048,1,72]{1,3,2,0:T(8,128)(2,1)} fusion(bf16[4,2048,1,72]{1,3,2,0:T(8,128)(2,1)} %get-tuple-element.84, s32[]{:T(128)} %get-tuple-element.83, f32[2048,2048]{0,1:T(8,128)} %get-tuple-element.77, f32[2048]{0:T(1024)S(1)} %fusion.41, f32[2048]{0:T(1024)S(1)} %get-tuple-element.78, ...), kind=kOutput, calls=%fused_computation.7.clone.1 | convolution fusion | flops 620904448 | bytes 17383936 | tf_op jit(solution)/shard_map/while/body/eval_jaxpr/hqk,khd->qhd/dot_general | solution.py:32
  218.4 29.2 %all-to-all-done.1 = bf16[4,2048,1,72]{3,0,2,1:T(4,128)(2,1)} async-done(((bf16[4,2048,1,72]{3,0,2,1:T(4,128)(2,1)}), bf16[4,2048,1,72]{3,0,2,1:T(4,128)(2,1)}, u32[]{:S(2)}, u32[]{:S(2)}) %all-to-all-start.1) | async-done | bytes 1179680 | tf_op jit(solution)/shard_map/all_to_all | solution.py:60
  256.9 9.7 %convolution_convert_fusion = bf16[512,3456]{1,0:T(8,128)(2,1)} fusion(bf16[512,1152]{1,0:T(8,128)(2,1)S(1)} %bitcast.91, bf16[1152,3456]{1,0:T(8,128)(2,1)} %param.13), kind=kOutput, calls=%fused_computation.15 | convolution fusion | flops 4078632960 | bytes 12681216 | tf_op jit(solution)/shard_map/dot_general | solution.py:21
  266.6 13.7 %reshape.105 = bf16[4,128,3,16,72]{4,3,2,1,0:T(8,128)(2,1)} reshape(bf16[512,3456]{1,0:T(8,128)(2,1)} %convolution_convert_fusion) | data formatting | bytes 7077888 | tf_op jit(solution)/shard_map/reshape | solution.py:22
  280.3 8.3 %copy.70 = bf16[4,128,3,16,72]{1,0,4,2,3:T(4,128)(2,1)} copy(bf16[4,128,3,16,72]{4,3,2,1,0:T(8,128)(2,1)} %reshape.105) | data formatting | bytes 7077888 | tf_op jit(solution)/shard_map/reshape | solution.py:22
  288.6 47.7 %all_to_all.66 = bf16[4,128,3,16,72]{1,0,4,2,3:T(4,128)(2,1)} all-to-all(bf16[4,128,3,16,72]{1,0,4,2,3:T(4,128)(2,1)} %copy.70), channel_id=1, replica_groups=mesh['frame'=8,'patch'=16] {'frame'}, dimensions={3} | all-to-all | bytes 7077888 | tf_op jit(solution)/shard_map/all_to_all | solution.py:74
  336.3 12.8 %copy.71 = bf16[4,128,3,8,2,72]{5,0,3,4,1,2:T(4,128)(2,1)} copy(bf16[4,128,3,8,2,72]{1,0,5,2,4,3:T(4,128)(2,1)} %bitcast.86) | data formatting | bytes 7077888 | tf_op jit(solution)/shard_map/all_to_all | solution.py:74
  352.5 9.6 %fusion.32 = (f32[128,2,32]{2,1,0:T(2,128)S(1)}, f32[128,2,32,32]{2,3,1,0:T(8,128)S(1)}) fusion(f32[128,2,32,32]{2,3,1,0:T(8,128)S(1)} %fusion.28), kind=kOutput, calls=%fused_computation.64 | output fusion | flops 1048607 | bytes 2129920 | tf_op jit(solution)/shard_map/sub | solution.py:42
  370.3 19.4 %all_to_all.67 = bf16[32,128,2,72]{1,3,2,0:T(8,128)(2,1)S(1)} all-to-all(bf16[32,128,2,72]{1,3,2,0:T(8,128)(2,1)} %copy.73), channel_id=1, replica_groups=mesh['frame'=8,'patch'=16] {'frame'}, dimensions={0} | all-to-all | bytes 2359296 | tf_op jit(solution)/shard_map/all_to_all | solution.py:65
  (43 shorter events, 71.4 us)
Async XLA Ops:
  0.0 251.7 %copy-start = (bf16[1152,1152]{1,0:T(8,128)(2,1)S(1)}, bf16[1152,1152]{1,0:T(8,128)(2,1)}, u32[]{:S(2)}) copy-start(bf16[1152,1152]{1,0:T(8,128)(2,1)} %param.11) | copy-start | bytes 7962628
  0.0 4.8 %copy-start.1 = (bf16[4,128,1152]{2,1,0:T(8,128)(2,1)S(1)}, bf16[4,128,1152]{2,1,0:T(8,128)(2,1)}, u32[]{:S(2)}) copy-start(bf16[4,128,1152]{2,1,0:T(8,128)(2,1)} %param.9) | copy-start | bytes 3538948
  37.0 54.3 %all-to-all-start = ((bf16[4,128,3,16,72]{1,0,4,2,3:T(4,128)(2,1)}), bf16[4,128,3,16,72]{1,0,4,2,3:T(4,128)(2,1)}, u32[]{:S(2)}, u32[]{:S(2)}) async-start(bf16[4,128,3,16,72]{1,0,4,2,3:T(4,128)(2,1)} %copy.62), calls=%async_computation | async-start | bytes 7077888 | tf_op jit(solution)/shard_map/all_to_all | solution.py:70
  212.0 6.3 %copy-start.5 = (f32[3,1152]{1,0:T(4,128)S(1)}, f32[3,1152]{1,0:T(4,128)}, u32[]{:S(2)}) copy-start(f32[3,1152]{1,0:T(4,128)} %param.15) | copy-start | bytes 41476
  212.0 35.6 %all-to-all-start.1 = ((bf16[4,2048,1,72]{3,0,2,1:T(4,128)(2,1)}), bf16[4,2048,1,72]{3,0,2,1:T(4,128)(2,1)}, u32[]{:S(2)}, u32[]{:S(2)}) async-start(bf16[4,2048,1,72]{3,0,2,1:T(4,128)(2,1)} %copy.65), calls=%async_computation.1 | async-start | bytes 4194304 | tf_op jit(solution)/shard_map/all_to_all | solution.py:60
  218.3 33.3 %copy-start.6 = (f32[1152]{0:T(1024)S(1)}, f32[1152]{0:T(1024)}, u32[]{:S(2)}) copy-start(f32[1152]{0:T(1024)} %get-tuple-element.41) | copy-start | bytes 13828
  255.4 1.0 copy-start.2
  370.3 19.5 %copy-start.3 = (bf16[4,128,1152]{2,1,0:T(8,128)(2,1)S(1)}, bf16[4,128,1152]{2,1,0:T(8,128)(2,1)}, u32[]{:S(2)}) copy-start(bf16[4,128,1152]{2,1,0:T(8,128)(2,1)} %copy-done.2) | copy-start | bytes 3538948
  370.3 19.5 %copy-start.4 = (bf16[1152,1152]{1,0:T(8,128)(2,1)S(1)}, bf16[1152,1152]{1,0:T(8,128)(2,1)}, u32[]{:S(2)}) copy-start(bf16[1152,1152]{1,0:T(8,128)(2,1)} %param.14) | copy-start | bytes 7962628
where the time goes:
time: 396 us; the launch traced here: 393 us
  matrix products  99 us (25%)
  local copies, waits for them, and re-layouts  86.6 us (22%)
  waiting for transfers between devices  76.6 us (19%)
  blocking collectives  67.1 us (17%)
  other arithmetic  50.1 us (13%)
  starting transfers between devices  13.2 us (3%)
    all_to_all x1, blocking collectives, shards(): lax.all_to_all(qkv_time, 'frame', split_axis=3, concat_axis=0, tiled=True)  47.7 us
    all_to_all x1, waiting for transfers between devices, shards(): lax.all_to_all(qkv, 'patch', split_axis=3, concat_axis=1, tiled=True)  47.5 us
    reshape x4, local copies, waits for them, and re-layouts, project_qkv(): return mixed.reshape(frames, patches, 3, HEADS, HD)  43.9 us
    reduce_sum x4, other arithmetic, spatial_frame(): probs = (expo / jnp.sum(expo, axis=-1, keepdims=True)).astype(jnp.bfloat16)  34.2 us
    dot_general x4, matrix products, spatial_frame(): jnp.einsum('hqk,khd->qhd', probs, qkv_frame[:, 2], preferred_element_type...  33.3 us
    dot_general x4, matrix products, spatial_frame(): jnp.einsum('qhd,khd->hqk', qkv_frame[:, 0], qkv_frame[:, 1], preferred_el...  32.4 us
    all_to_all x1, waiting for transfers between devices, spatial_items(): lax.all_to_all(attended, 'patch', split_axis=1, concat_axis=2, tiled=True)  29.2 us
    dot_general x2, matrix products, project_qkv(): jnp.dot(normed, weight, preferred_element_type=jnp.float32)  19.4 us
  transfers between devices with their start and end apart: 2, of which 2 were waited for; matrix products, arithmetic and copies ran while one was open for 0% of the time, Pallas kernels for 0%

commit v1 on v0

v1 whole, which is shorter than its diff:
```python
import functools

import jax
import jax.numpy as jnp
from jax import lax
from jax.experimental import pallas as pl
from jax.experimental.pallas import tpu as pltpu
from jax.sharding import PartitionSpec as P

HEADS = 16
HD = 72
D = 1152
WIN = 384
ROWS = 2048
QT = 256
SCALE = HD ** (-0.5) * 1.4426950408889634
MESH = pl.DeviceIdType.MESH
VMEM = pl.BlockSpec(memory_space=pltpu.VMEM)
ANY = pl.BlockSpec(memory_space=pl.ANY)
BF = jnp.bfloat16
F32 = jnp.float32


def params(collective_id=None):
    return pltpu.CompilerParams(
        collective_id=collective_id,
        has_side_effects=collective_id is not None,
        vmem_limit_bytes=56 * 2**20,
    )


def remote(src, dst, send_sem, recv_sem, device):
    return pltpu.make_async_remote_copy(
        src_ref=src, dst_ref=dst, send_sem=send_sem, recv_sem=recv_sem, device_id=device, device_id_type=MESH
    )


def meet(devices):
    barrier = pltpu.get_barrier_semaphore()
    for device in devices:
        pl.semaphore_signal(barrier, inc=1, device_id=device, device_id_type=MESH)
    pl.semaphore_wait(barrier, len(devices))


def modulate(values, mod_ref):
    mean = jnp.mean(values, axis=-1, keepdims=True)
    centered = values - mean
    var = jnp.mean(centered * centered, axis=-1, keepdims=True)
    return (centered * lax.rsqrt(var + 1e-06) * (1.0 + mod_ref[1:2, :]) + mod_ref[0:1, :]).astype(BF)


def place():
    frame, patch = lax.axis_index("frame"), lax.axis_index("patch")
    return frame, patch, patch // 8, (patch // 2) % 4, patch % 2


def rows16(index):
    return pl.ds(pl.multiple_of(index * 16, 16), 16)


def gather_kernel(tok, mod, full, tok_t, hs, zbuf, xs, xr, zs, zr, ls, ts, tr):
    frame, patch, zh, x, core = place()
    zpatch = (1 - zh) * 8 + x * 2 + core
    sibling = (frame, patch + 1 - 2 * core)
    zdev = (frame, zpatch)
    xpos = [(x + dx) % 4 for dx in (1, 3, 2)]
    xdev = [(frame, zh * 8 + p * 2 + core) for p in xpos]
    others = [((frame + d) % 8, patch) for d in range(1, 8)]
    meet([sibling, zdev] + xdev + others)

    def norm(f):
        hs[f] = modulate(tok[f].astype(F32), mod)

    copies = []
    for j in range(2):
        norm(2 * (1 - zh) + j)
        copies.append(remote(hs.at[2 * (1 - zh) + j], zbuf.at[j], zs.at[j], zr.at[j], zdev))
        copies[-1].start()
    for j in range(2):
        norm(2 * zh + j)
    for i, device in enumerate(xdev):
        copies.append(remote(hs.at[2 * zh + xpos[i] // 2], full.at[patch], xs.at[i], xr.at[patch], device))
        copies[-1].start()
    own = pltpu.make_async_copy(hs.at[2 * zh + x // 2], full.at[patch], ls.at[0])
    own.start()
    for i, device in enumerate(others):
        copies.append(remote(tok.at[:, rows16(device[0]), :], tok_t.at[frame], ts.at[i], tr.at[i], device))
        copies[-1].start()
    mine = pltpu.make_async_copy(tok.at[:, rows16(frame), :], tok_t.at[frame], ls.at[1])
    mine.start()
    own.wait()

    def relay(source, slot):
        copies.append(remote(full.at[source], full.at[source], xs.at[slot], xr.at[source], sibling))
        copies[-1].start()

    def arrived(source, device):
        remote(full.at[source], full.at[source], xs.at[0], xr.at[source], device).wait_recv()

    relay(patch, 6)
    for j in range(2):
        remote(zbuf.at[j], zbuf.at[j], zs.at[j], zr.at[j], zdev).wait_recv()
    for i, device in enumerate(xdev):
        copies.append(remote(zbuf.at[xpos[i] // 2], full.at[zpatch], xs.at[3 + i], xr.at[zpatch], device))
        copies[-1].start()
    own = pltpu.make_async_copy(zbuf.at[x // 2], full.at[zpatch], ls.at[0])
    own.start()
    own.wait()
    relay(zpatch, 7)
    for i, device in enumerate(xdev):
        arrived(device[1], device)
        relay(device[1], 8 + i)
    for i, device in enumerate(xdev):
        source = (1 - zh) * 8 + xpos[i] * 2 + core
        arrived(source, device)
        relay(source, 11 + i)
    for i in range(16):
        source = (i // 2) * 2 + 1 - core
        if i % 2 == 0:
            arrived(source, sibling)
    mine.wait()
    for i, device in enumerate(others):
        remote(tok_t.at[frame], tok_t.at[frame], ts.at[i], tr.at[6 - i], device).wait_recv()
    for copy in copies:
        copy.wait_send()


def gather(tokens, mod):
    return pl.pallas_call(
        gather_kernel,
        name="gather",
        out_shape=[jax.ShapeDtypeStruct((16, 128, D), BF), jax.ShapeDtypeStruct((8, 4, 16, D), BF)],
        in_specs=[VMEM, VMEM],
        out_specs=[VMEM, VMEM],
        scratch_shapes=[
            pltpu.VMEM((4, 128, D), BF),
            pltpu.VMEM((2, 128, D), BF),
            pltpu.SemaphoreType.DMA((14,)),
            pltpu.SemaphoreType.DMA((16,)),
            pltpu.SemaphoreType.DMA((2,)),
            pltpu.SemaphoreType.DMA((2,)),
            pltpu.SemaphoreType.DMA((2,)),
            pltpu.SemaphoreType.DMA((7,)),
            pltpu.SemaphoreType.DMA((7,)),
        ],
        compiler_params=params(1),
    )(tokens, mod)


ONE_LANE = (255, 255, 255, 0)


def head_lanes(shape, head, group):
    lane = lax.broadcasted_iota(jnp.int32, shape, 1) + (head // 2) * 128
    low = 32 * group + HD * head
    return (lane >= low) & (lane < low + HD)


def project(h, w, qkv, vals, chunk, group):
    rows = pl.ds(pl.multiple_of(chunk * QT, QT), QT)
    for part in range(3):
        cols = slice(part * WIN, (part + 1) * WIN)
        acc = jnp.dot(h, w[:, cols], preferred_element_type=F32)
        if part == 0:
            acc = acc * SCALE
        if part < 2:
            qkv[rows, cols] = acc.astype(BF)
        else:
            for head in range(4):
                base = (head // 2) * 128
                keep = head_lanes((QT, 256), head, group)
                lane = lax.broadcasted_iota(jnp.int32, (QT, 256), 1)
                one = jnp.where(lane == ONE_LANE[head], 1.0, 0.0)
                vals[head, rows, :] = jnp.where(keep, acc[:, base : base + 256], one).astype(BF)


def attend(qkv, vals, out, tile, group):
    rows = pl.ds(pl.multiple_of(tile * QT, QT), QT)
    halves = []
    for head in range(4):
        base = (head // 2) * 128
        keep = head_lanes((QT, 256), head, group)
        query = jnp.where(keep, qkv[rows, base : base + 256], jnp.zeros((), BF))
        keys = qkv[:, WIN + base : WIN + base + 256]
        scores = lax.dot_general(query, keys, (((1,), (1,)), ((), ())), preferred_element_type=F32)
        top = jnp.max(scores, axis=-1, keepdims=True)
        probs = jnp.exp2(scores - top).astype(BF)
        mixed = jnp.dot(probs, vals[head], preferred_element_type=F32)
        lane = ONE_LANE[head]
        halves.append(jnp.where(keep, mixed / mixed[:, lane : lane + 1], 0.0))
    first, second = halves[0] + halves[1], halves[2] + halves[3]
    out[rows, 0:128] = first[:, :128].astype(BF)
    out[rows, 128:256] = (first[:, 128:] + second[:, :128]).astype(BF)
    out[rows, 256:384] = second[:, 128:].astype(BF)


def load_window(w, wbuf, sems, group):
    copies = []
    for part in range(3):
        cols = pl.ds(pl.multiple_of(part * D + 256 * group, 128), WIN)
        copies.append(pltpu.make_async_copy(w.at[:, cols], wbuf.at[:, pl.ds(part * WIN, WIN)], sems.at[part]))
        copies[-1].start()
    return copies


def spatial_kernel(full, w, out, wbuf, qkv, vals, sems):
    frame, patch, zh, x, core = place()
    group = (x % 2) * 2 + core
    for copy in load_window(w, wbuf, sems, group):
        copy.wait()

    def proj(i, _):
        h = full[pl.ds(i * 2, 2)].reshape(QT, D)
        project(h, wbuf, qkv, vals, i, group)
        return 0

    lax.fori_loop(0, ROWS // QT, proj, 0)

    def att(i, _):
        attend(qkv, vals, out, i, group)
        return 0

    lax.fori_loop(0, ROWS // QT, att, 0)


def spatial(full, w):
    return pl.pallas_call(
        spatial_kernel,
        name="spatial",
        out_shape=jax.ShapeDtypeStruct((ROWS, WIN), BF),
        in_specs=[VMEM, ANY],
        out_specs=VMEM,
        scratch_shapes=[
            pltpu.VMEM((D, 3 * WIN), BF),
            pltpu.VMEM((ROWS, 2 * WIN), BF),
            pltpu.VMEM((4, ROWS, 256), BF),
            pltpu.SemaphoreType.DMA((3,)),
        ],
        compiler_params=params(),
    )(full, w)


def meet_all(frame, patch):
    barrier = pltpu.get_barrier_semaphore()

    def signal(i, _):
        device = ((frame + i // 16) % 8, (patch + i % 16) % 16)
        pl.semaphore_signal(barrier, inc=1, device_id=device, device_id_type=MESH)
        return 0

    lax.fori_loop(1, 128, signal, 0)
    pl.semaphore_wait(barrier, 127)


def spread_kernel(att, att_t, send, recv):
    frame, patch, zh, x, core = place()
    group = (x % 2) * 2 + core
    at = frame * 4 + zh * 2 + x // 2
    meet_all(frame, patch)

    def go(i, _):
        i = (i * 51) % 128
        f, p = (frame + i // 16) % 8, (patch + i % 16) % 16
        remote(att.at[rows16(p * 8 + f), :], att_t.at[group, at], send, recv, (f, p)).start()
        return 0

    lax.fori_loop(1, 128, go, 0)
    pltpu.make_async_copy(att.at[rows16(patch * 8 + frame), :], att_t.at[group, at], recv).start()
    pltpu.make_async_copy(att_t, att_t, recv).wait()
    pltpu.make_async_copy(att.at[pl.ds(0, 2032), :], att.at[pl.ds(0, 2032), :], send).wait()


def spread(att):
    return pl.pallas_call(
        spread_kernel,
        name="spread",
        out_shape=jax.ShapeDtypeStruct((4, 32, 16, WIN), BF),
        in_specs=[VMEM],
        out_specs=VMEM,
        scratch_shapes=[pltpu.SemaphoreType.DMA, pltpu.SemaphoreType.DMA],
        compiler_params=params(2),
    )(att)


def swap_rows(forward):
    row = lax.broadcasted_iota(jnp.int32, (512, 512), 0)
    col = lax.broadcasted_iota(jnp.int32, (512, 512), 1)
    if forward:
        return jnp.where(col == (row % 32) * 16 + row // 32, 1.0, 0.0).astype(BF)
    return jnp.where(col == (row % 16) * 32 + row // 16, 1.0, 0.0).astype(BF)


def temporal_kernel(
    att_t, tok, w_out_s, mod_s, w_qkv, w_out, mod, out, wo_s, wq, wo, att, mid, hp, qkv, mixed_all, sems
):
    loads = [
        pltpu.make_async_copy(src, dst, sems.at[i])
        for i, (src, dst) in enumerate([(w_out_s, wo_s), (w_qkv, wq), (w_out, wo)])
    ]
    for load in loads:
        load.start()
    for tile in range(9):
        cols = slice(tile * 128, tile * 128 + 128)
        group, rest = min(tile // 2, 3), tile - 2 * min(tile // 2, 3)
        part = att_t[group, :, :, rest * 128 : rest * 128 + 128].reshape(512, 128)
        if rest == 0 and group > 0:
            part = part + att_t[group - 1, :, :, 256:384].reshape(512, 128)
        att[:, cols] = part
    loads[0].wait()

    def finish_mid(i, _):
        rows = pl.ds(pl.multiple_of(i * 128, 128), 128)
        proj = jnp.dot(att[rows, :], wo_s[...], preferred_element_type=F32)
        values = (tok[rows, :].astype(F32) + mod_s[2:3, :] * proj).astype(BF)
        mid[rows, :] = values
        att[rows, :] = modulate(values.astype(F32), mod)
        return 0

    lax.fori_loop(0, 4, finish_mid, 0)
    hp[...] = jnp.dot(swap_rows(True), att[...], preferred_element_type=F32).astype(BF)
    loads[1].wait()
    for part in range(9):
        cols = slice(part * WIN, (part + 1) * WIN)
        acc = jnp.dot(hp[...], wq[:, cols], preferred_element_type=F32)
        if part < 3:
            acc = acc * SCALE
        qkv[:, cols] = acc.astype(BF)

    row = lax.broadcasted_iota(jnp.int32, (128, 128), 0)
    col = lax.broadcasted_iota(jnp.int32, (128, 128), 1)
    same = row // 32 == col // 32
    lane = lax.broadcasted_iota(jnp.int32, (128, 256), 1)

    def group(i, _):
        rows = pl.ds(pl.multiple_of(i * 128, 128), 128)
        for head in range(HEADS):
            base = min(head * HD // 128, 7) * 128
            low = head * HD - base
            keep = (lane >= low) & (lane < low + HD)
            query = jnp.where(keep, qkv[rows, base : base + 256], jnp.zeros((), BF))
            keys = qkv[rows, D + base : D + base + 256]
            scores = lax.dot_general(query, keys, (((1,), (1,)), ((), ())), preferred_element_type=F32)
            scores = jnp.where(same, scores, -1e30)
            top = jnp.max(scores, axis=-1, keepdims=True)
            expo = jnp.exp2(scores - top)
            probs = (expo / jnp.sum(expo, axis=-1, keepdims=True)).astype(BF)
            mixed = jnp.dot(probs, qkv[rows, 2 * D + base : 2 * D + base + 256], preferred_element_type=F32)
            mixed = mixed.astype(BF)
            if low == 0:
                mixed_all[rows, base : base + 256] = mixed
            else:
                mixed_all[rows, base : base + 256] = jnp.where(keep, mixed, mixed_all[rows, base : base + 256])
        return 0

    lax.fori_loop(0, 4, group, 0)
    att[...] = jnp.dot(swap_rows(False), mixed_all[...], preferred_element_type=F32).astype(BF)
    loads[2].wait()

    def finish(i, _):
        rows = pl.ds(pl.multiple_of(i * 128, 128), 128)
        proj = jnp.dot(att[rows, :], wo[...], preferred_element_type=F32)
        out[rows, :] = (mid[rows, :].astype(F32) + mod[2:3, :] * proj).astype(BF)
        return 0

    lax.fori_loop(0, 4, finish, 0)


def temporal(att_t, tok_t, w_out_s, mod_s, w_qkv, w_out, mod):
    return pl.pallas_call(
        temporal_kernel,
        name="temporal",
        out_shape=jax.ShapeDtypeStruct((512, D), BF),
        in_specs=[VMEM, VMEM, ANY, VMEM, ANY, ANY, VMEM],
        out_specs=VMEM,
        scratch_shapes=[
            pltpu.VMEM((D, D), BF),
            pltpu.VMEM((D, 3 * D), BF),
            pltpu.VMEM((D, D), BF),
            pltpu.VMEM((512, D), BF),
            pltpu.VMEM((512, D), BF),
            pltpu.VMEM((512, D), BF),
            pltpu.VMEM((512, 3 * D), BF),
            pltpu.VMEM((512, D), BF),
            pltpu.SemaphoreType.DMA((3,)),
        ],
        compiler_params=params(),
    )(att_t, tok_t, w_out_s, mod_s, w_qkv, w_out, mod)


def home_kernel(done, out, ss, rs, ls):
    frame, patch, zh, x, core = place()
    others = [((frame + d) % 8, patch) for d in range(1, 8)]
    meet(others)
    copies = []
    for i, device in enumerate(others):
        copies.append(remote(done.at[device[0]], out.at[:, rows16(frame), :], ss.at[i], rs.at[i], device))
        copies[-1].start()
    mine = pltpu.make_async_copy(done.at[frame], out.at[:, rows16(frame), :], ls)
    mine.start()
    mine.wait()
    for copy in copies:
        copy.wait()


def home(done):
    return pl.pallas_call(
        home_kernel,
        name="home",
        out_shape=jax.ShapeDtypeStruct((4, 128, D), BF),
        in_specs=[VMEM],
        out_specs=VMEM,
        scratch_shapes=[
            pltpu.SemaphoreType.DMA((7,)),
            pltpu.SemaphoreType.DMA((7,)),
            pltpu.SemaphoreType.DMA,
        ],
        compiler_params=params(3),
    )(done)


def shards(tokens, w_qkv_s, w_out_s, mod_s, w_qkv_t, w_out_t, mod_t):
    full, tok_t = gather(tokens, mod_s)
    att = spatial(full, w_qkv_s)
    att_t = spread(att)
    done = temporal(att_t, tok_t.reshape(512, D), w_out_s, mod_s, w_qkv_t, w_out_t, mod_t)
    return home(done.reshape(8, 4, 16, D))


def solution(mesh):
    return jax.shard_map(
        shards,
        mesh=mesh,
        in_specs=(P("frame", "patch", None), P(), P(), P(), P(), P(), P()),
        out_specs=P("frame", "patch", None),
        check_vma=False,
    )
```

time: 396 us -> 171 us (0.43)
  Pallas kernels: 0 us -> 167 us
  matrix products: 99 us -> 0 us
  local copies, waits for them, and re-layouts: 86.6 us -> 2.37 us
  waiting for transfers between devices: 76.6 us -> 0 us
  blocking collectives: 67.1 us -> 0 us
  other arithmetic: 50.1 us -> 0 us
  starting transfers between devices: 13.2 us -> 0 us
    pallas_call x0 -> x5, Pallas kernels: none -> 167 us  [the longest x1 49.8 us: gather(): pl.pallas_call(gather_kernel, name='gather', out_shape=[jax.ShapeDtypeStr...]
    dot_general x14 -> x0, matrix products: 99 us -> none  [the longest x4 33.3 us: spatial_frame(): jnp.einsum('hqk,khd->qhd', probs, qkv_frame[:, 2], preferred_element_type...]
    all_to_all x2 -> x0, waiting for transfers between devices: 76.6 us -> none  [the longest x1 47.5 us: shards(): lax.all_to_all(qkv, 'patch', split_axis=3, concat_axis=1, tiled=True)]
    all_to_all x2 -> x0, blocking collectives: 67.1 us -> none  [the longest x1 47.7 us: shards(): lax.all_to_all(qkv_time, 'frame', split_axis=3, concat_axis=0, tiled=True)]
    reshape x4 -> x0, local copies, waits for them, and re-layouts: 43.9 us -> none  [project_qkv(): return mixed.reshape(frames, patches, 3, HEADS, HD)]
    reduce_sum x7 -> x0, other arithmetic: 37.9 us -> none  [the longest x4 34.2 us: spatial_frame(): probs = (expo / jnp.sum(expo, axis=-1, keepdims=True)).astype(jnp.bfloat16)]
    all_to_all x5 -> x0, local copies, waits for them, and re-layouts: 28.7 us -> none  [the longest x1 12.8 us: shards(): lax.all_to_all(qkv_time, 'frame', split_axis=3, concat_axis=0, tiled=True)]
    all_to_all x2 -> x0, starting transfers between devices: 13.2 us -> none  [the longest x1 6.87 us: shards(): lax.all_to_all(qkv, 'patch', split_axis=3, concat_axis=1, tiled=True)]
  transfers between devices with their start and end apart: 2 -> 0, of which waited for: 2 -> 0; matrix products, arithmetic and copies ran while one was open for 0% -> 0% of each run, Pallas kernels for 0% -> 0%
where the time goes in v1:
time: 171 us; the launch traced here: 169 us
  Pallas kernels  167 us (98%)
  local copies, waits for them, and re-layouts  2.37 us (1%)
    pallas_call x1, Pallas kernels, gather(): pl.pallas_call(gather_kernel, name='gather', out_shape=[jax.ShapeDtypeStr...  49.8 us
    pallas_call x1, Pallas kernels, spatial(): pl.pallas_call(spatial_kernel, name='spatial', out_shape=jax.ShapeDtypeSt...  40.4 us
    pallas_call x1, Pallas kernels, spread(): pl.pallas_call(spread_kernel, name='spread', out_shape=jax.ShapeDtypeStru...  30.5 us
    pallas_call x1, Pallas kernels, temporal(): pl.pallas_call(temporal_kernel, name='temporal', out_shape=jax.ShapeDtype...  24.9 us
    pallas_call x1, Pallas kernels, home(): pl.pallas_call(home_kernel, name='home', out_shape=jax.ShapeDtypeStruct((...  21.4 us

profile of v1, /device:TPU:32, one launch (start us, length us, event | category | flops | bytes accessed | tf_op | source)
XLA Modules:
  0.0 169.4 jit_solution(12568084912252900535)
XLA Ops:
  0.0 49.8 %gather.1 = (bf16[16,128,1152]{2,1,0:T(8,128)(2,1)}, bf16[8,4,16,1152]{3,2,1,0:T(8,128)(2,1)}) custom-call(bf16[4,128,1152]{2,1,0:T(8,128)(2,1)} %tok.1, f32[3,1152]{1,0:T(4,128)} %mod_s.1), custom_call_target="tpu_custom_call" | custom-call | tf_op jit(solution)/shard_map/gather/pallas_call | solution.py:129
  49.8 40.4 %spatial.1.att = bf16[2048,384]{1,0:T(8,128)(2,1)} custom-call(bf16[16,128,1152]{2,1,0:T(8,128)(2,1)} %get-tuple-element.7.full, bf16[1152,3456]{1,0:T(8,128)(2,1)} %w.1), custom_call_target="tpu_custom_call" | custom-call | tf_op jit(solution)/shard_map/spatial/pallas_call | solution.py:227
  90.3 30.5 %spread.1.att_t = bf16[4,32,16,384]{3,2,1,0:T(8,128)(2,1)} custom-call(bf16[2048,384]{1,0:T(8,128)(2,1)} %spatial.1.att), custom_call_target="tpu_custom_call" | custom-call | tf_op jit(solution)/shard_map/spread/pallas_call | solution.py:274
  120.7 24.9 %temporal.1 = bf16[512,1152]{1,0:T(8,128)(2,1)} custom-call(bf16[4,32,16,384]{3,2,1,0:T(8,128)(2,1)} %spread.1.att_t, bf16[512,1152]{1,0:T(8,128)(2,1)} %bitcast.3, bf16[1152,1152]{1,0:T(8,128)(2,1)} %w_out_s.1, f32[3,1152]{1,0:T(4,128)} %mod_s.1, bf16[1152,3456]{1,0:T(8,128)(2,1)} %w_qkv.1, bf16[1152,1152]{1,0:T(8,128)(2,1)} %w_out.1, f32[3,1152]{1,0:T(4,128)} %mod.3), custom_call_target="tpu_custom_call" | custom-call | tf_op jit(solution)/shard_map/temporal/pallas_call | solution.py:369
  145.6 21.4 %home.1 = bf16[4,128,1152]{2,1,0:T(8,128)(2,1)} custom-call(bf16[8,4,16,1152]{3,2,1,0:T(8,128)(2,1)} %bitcast.2), custom_call_target="tpu_custom_call" | custom-call | tf_op jit(solution)/shard_map/home/pallas_call | solution.py:406
  167.0 2.4 %copy.9 = bf16[4,128,1152]{2,1,0:T(8,128)(2,1)} copy(bf16[4,128,1152]{2,1,0:T(8,128)(2,1)} %home.1) | data formatting | bytes 2359296

commit v2 on v0

v2 whole, which is shorter than its diff:
```python
import functools

import jax
import jax.numpy as jnp
from jax import lax
from jax.experimental import pallas as pl
from jax.experimental.pallas import tpu as pltpu
from jax.sharding import PartitionSpec as P

HEADS = 16
HD = 72
D = 1152
WIN = 384
ROWS = 2048
QT = 256
KC = 256
SCALE = HD ** (-0.5) * 1.4426950408889634
MESH = pl.DeviceIdType.MESH
VMEM = pl.BlockSpec(memory_space=pltpu.VMEM)
ANY = pl.BlockSpec(memory_space=pl.ANY)
BF = jnp.bfloat16
F32 = jnp.float32


def params(collective_id=None):
    return pltpu.CompilerParams(
        collective_id=collective_id,
        has_side_effects=collective_id is not None,
        vmem_limit_bytes=56 * 2**20,
    )


def remote(src, dst, send_sem, recv_sem, device):
    return pltpu.make_async_remote_copy(
        src_ref=src, dst_ref=dst, send_sem=send_sem, recv_sem=recv_sem, device_id=device, device_id_type=MESH
    )


def modulate(values, mod_ref):
    mean = jnp.mean(values, axis=-1, keepdims=True)
    centered = values - mean
    var = jnp.mean(centered * centered, axis=-1, keepdims=True)
    return (centered * lax.rsqrt(var + 1e-06) * (1.0 + mod_ref[1:2, :]) + mod_ref[0:1, :]).astype(BF)


def place():
    frame, patch = lax.axis_index("frame"), lax.axis_index("patch")
    return frame, patch, patch // 8, (patch // 2) % 4, patch % 2


def rows16(index):
    return pl.ds(pl.multiple_of(index * 16, 16), 16)


def head_lanes(shape, head, group):
    lane = lax.broadcasted_iota(jnp.int32, shape, 1) + (head // 2) * 128
    low = 32 * group + HD * head
    return (lane >= low) & (lane < low + HD)


def project(h, w, qk, vt, vwide, index, group):
    rows = pl.ds(pl.multiple_of(index * QT, QT), QT)
    for part in range(3):
        cols = slice(part * WIN, (part + 1) * WIN)
        acc = jnp.dot(h, w[:, cols], preferred_element_type=F32)
        if part == 0:
            acc = acc * SCALE
        if part < 2:
            qk[rows, cols] = acc.astype(BF)
        else:
            vwide[...] = acc.T
    one = jnp.where(lax.broadcasted_iota(jnp.int32, (8, QT), 0) == 0, 1.0, 0.0)
    for head in range(4):
        part = vwide[pl.ds(pl.multiple_of(32 * group + HD * head, 8), HD), :]
        vt[head, :, rows] = jnp.concatenate([part, one], axis=0).astype(BF)


def load_window(w, wbuf, sems, group):
    copies = []
    for part in range(3):
        cols = pl.ds(pl.multiple_of(part * D + 256 * group, 128), WIN)
        copies.append(pltpu.make_async_copy(w.at[:, cols], wbuf.at[:, pl.ds(part * WIN, WIN)], sems.at[part]))
        copies[-1].start()
    return copies


def swap_rows(forward):
    row = lax.broadcasted_iota(jnp.int32, (512, 512), 0)
    col = lax.broadcasted_iota(jnp.int32, (512, 512), 1)
    if forward:
        return jnp.where(col == (row % 32) * 16 + row // 32, 1.0, 0.0).astype(BF)
    return jnp.where(col == (row % 16) * 32 + row // 16, 1.0, 0.0).astype(BF)


def fused_kernel(
    tok, mod_s, mod_t, w_qkv_s, w_out_s, w_qkv_t, w_out_t, out,
    hs, zbuf, full, wbuf, qk, vt, vwide, s0, s1, m0, m1, awide, att, att_t, tok_t, wo_s, wq, wo,
    flat, mid, hp, qkv, mixed_all, done,
    w_sem, z_sem, full_sem, gather_send, tok_send, tok_recv, att_send, att_recv, home_send, home_recv,
):
    frame, patch, zh, x, core = place()
    group = (x % 2) * 2 + core
    at = frame * 4 + zh * 2 + x // 2
    zpatch = (1 - zh) * 8 + x * 2 + core
    sibling = (frame, patch + 1 - 2 * core)
    zdev = (frame, zpatch)

    barrier = pltpu.get_barrier_semaphore()

    def signal(i, _):
        device = ((frame + i // 16) % 8, (patch + i % 16) % 16)
        pl.semaphore_signal(barrier, inc=1, device_id=device, device_id_type=MESH)
        return 0

    lax.fori_loop(1, 128, signal, 0)
    windows = load_window(w_qkv_s, wbuf, w_sem, group)
    loads = [
        pltpu.make_async_copy(src, dst, w_sem.at[3 + i])
        for i, (src, dst) in enumerate([(w_out_s, wo_s), (w_qkv_t, wq), (w_out_t, wo)])
    ]
    for load in loads:
        load.start()

    def norm(f):
        hs[f] = modulate(tok[f].astype(F32), mod_s)

    norm(2 * (1 - zh))
    norm(2 * (1 - zh) + 1)
    pl.semaphore_wait(barrier, 127)
    for j in range(2):
        remote(hs.at[2 * (1 - zh) + j], zbuf.at[j], gather_send, z_sem.at[j], zdev).start()
    norm(2 * zh)
    norm(2 * zh + 1)

    def along_x(chunk, source):
        for d in (1, 3, 2):
            xd = (x + d) % 4
            remote(chunk(xd // 2), full.at[source], gather_send, full_sem.at[source], (frame, zh * 8 + xd * 2 + core)).start()
        pltpu.make_async_copy(chunk(x // 2), full.at[source], full_sem.at[source]).start()

    along_x(lambda j: hs.at[2 * zh + j], patch)
    awide[...] = jnp.zeros_like(awide)
    for window in windows:
        window.wait()

    def arrived(source):
        pltpu.make_async_copy(full.at[source], full.at[source], full_sem.at[source]).wait()

    def chip(k, _):
        plane = (zh + k // 4) % 2
        index = plane * 4 + (x + k % 4) % 4
        source = index * 2 + core
        arrived(source)
        remote(full.at[source], full.at[source], gather_send, full_sem.at[source], sibling).start()
        arrived(index * 2 + 1 - core)
        h = full[pl.ds(index * 2, 2)].reshape(QT, D)
        project(h, wbuf, qk, vt, vwide, index, group)
        return 0

    chip(0, 0)
    for j in range(2):
        pltpu.make_async_copy(zbuf.at[j], zbuf.at[j], z_sem.at[j]).wait()
    along_x(lambda j: zbuf.at[j], zpatch)

    def tokens_out(d, _):
        f = (frame + d) % 8
        remote(tok.at[:, rows16(f), :], tok_t.at[frame], tok_send, tok_recv, (f, patch)).start()
        return 0

    lax.fori_loop(1, 8, tokens_out, 0)
    pltpu.make_async_copy(tok.at[:, rows16(frame), :], tok_t.at[frame], tok_recv).start()
    lax.fori_loop(1, 8, chip, 0)

    scores, tops = (s0, s1), (m0, m1)
    first = patch // 2

    def score(head, tile, slot):
        base = (head // 2) * 128
        rows = pl.ds(pl.multiple_of(tile * QT, QT), QT)
        keep = head_lanes((QT, 256), head, group)
        query = jnp.where(keep, qk[rows, base : base + 256], jnp.zeros((), BF))
        top = None
        for c in range(ROWS // KC):
            keys = qk[c * KC : (c + 1) * KC, WIN + base : WIN + base + 256]
            part = lax.dot_general(keys, query, (((1,), (1,)), ((), ())), preferred_element_type=F32)
            scores[slot][c * KC : (c + 1) * KC, :] = part
            part = jnp.max(part.reshape(KC // 8, 8, QT), axis=0)
            top = part if top is None else jnp.maximum(top, part)
        tops[slot][...] = jnp.broadcast_to(jnp.max(top, axis=0, keepdims=True), (8, QT))

    def mix(head, slot):
        top = tops[slot][0:1, :]
        acc = None
        for c in range(ROWS // KC):
            span = slice(c * KC, (c + 1) * KC)
            probs = jnp.exp2(scores[slot][span, :] - top).astype(BF)
            part = jnp.dot(vt[head, :, span], probs, preferred_element_type=F32)
            acc = part if acc is None else acc + part
        awide[pl.ds(pl.multiple_of(32 * group + HD * head, 8), HD), :] = acc[:HD] / acc[HD : HD + 1]

    score(0, first, 0)

    def attend(i, _):
        tile = (first + i) % 8
        for head in range(4):
            score((head + 1) % 4, tile if head < 3 else (first + i + 1) % 8, (head + 1) % 2)
            mix(head, head % 2)
        att[pl.ds(pl.multiple_of(tile * QT, QT), QT), :] = awide[...].T.astype(BF)

        def go(n, _):
            f, p = n // 2, tile * 2 + n % 2
            src, dst = att.at[rows16(p * 8 + f), :], att_t.at[group, at]
            mine = (f == frame) & (p == patch)

            @pl.when(jnp.logical_not(mine))
            def _():
                remote(src, dst, att_send, att_recv, (f, p)).start()

            @pl.when(mine)
            def _():
                pltpu.make_async_copy(src, dst, att_recv).start()

            return 0

        lax.fori_loop(0, 16, go, 0)
        return 0

    lax.fori_loop(0, 8, attend, 0)

    for load in loads:
        load.wait()
    pltpu.make_async_copy(tok_t, tok_t, tok_recv).wait()
    pltpu.make_async_copy(att_t, att_t, att_recv).wait()
    for tile in range(9):
        cols = slice(tile * 128, tile * 128 + 128)
        g, rest = min(tile // 2, 3), tile - 2 * min(tile // 2, 3)
        part = att_t[g, :, :, rest * 128 : rest * 128 + 128].reshape(512, 128)
        if rest == 0 and g > 0:
            part = part + att_t[g - 1, :, :, 256:384].reshape(512, 128)
        flat[:, cols] = part

    def finish_mid(i, _):
        rows = pl.ds(pl.multiple_of(i * 256, 256), 256)
        proj = jnp.dot(flat[rows, :], wo_s[...], preferred_element_type=F32)
        values = tok_t[pl.ds(i * 4, 4)].reshape(256, D).astype(F32)
        values = (values + mod_s[2:3, :] * proj).astype(BF)
        mid[rows, :] = values
        flat[rows, :] = modulate(values.astype(F32), mod_t)
        return 0

    lax.fori_loop(0, 2, finish_mid, 0)
    hp[...] = jnp.dot(swap_rows(True), flat[...], preferred_element_type=F32).astype(BF)
    for part in range(9):
        cols = slice(part * WIN, (part + 1) * WIN)
        acc = jnp.dot(hp[...], wq[:, cols], preferred_element_type=F32)
        if part < 3:
            acc = acc * SCALE
        qkv[:, cols] = acc.astype(BF)

    row = lax.broadcasted_iota(jnp.int32, (128, 128), 0)
    col = lax.broadcasted_iota(jnp.int32, (128, 128), 1)
    same = row // 32 == col // 32
    lane = lax.broadcasted_iota(jnp.int32, (128, 256), 1)

    def four_patches(i, _):
        rows = pl.ds(pl.multiple_of(i * 128, 128), 128)
        for head in range(HEADS):
            base = min(head * HD // 128, 7) * 128
            low = head * HD - base
            keep = (lane >= low) & (lane < low + HD)
            query = jnp.where(keep, qkv[rows, base : base + 256], jnp.zeros((), BF))
            keys = qkv[rows, D + base : D + base + 256]
            part = lax.dot_general(query, keys, (((1,), (1,)), ((), ())), preferred_element_type=F32)
            part = jnp.where(same, part, -1e30)
            expo = jnp.exp2(part - jnp.max(part, axis=-1, keepdims=True))
            probs = (expo / jnp.sum(expo, axis=-1, keepdims=True)).astype(BF)
            mixed = jnp.dot(probs, qkv[rows, 2 * D + base : 2 * D + base + 256], preferred_element_type=F32)
            mixed = mixed.astype(BF)
            if low == 0:
                mixed_all[rows, base : base + 256] = mixed
            else:
                mixed_all[rows, base : base + 256] = jnp.where(keep, mixed, mixed_all[rows, base : base + 256])
        return 0

    lax.fori_loop(0, 4, four_patches, 0)
    flat[...] = jnp.dot(swap_rows(False), mixed_all[...], preferred_element_type=F32).astype(BF)

    def finish(i, _):
        i = (frame // 2 + i) % 4
        rows = pl.ds(pl.multiple_of(i * 128, 128), 128)
        proj = jnp.dot(flat[rows, :], wo[...], preferred_element_type=F32)
        values = (mid[rows, :].astype(F32) + mod_t[2:3, :] * proj).astype(BF)
        done[pl.ds(i * 2, 2)] = values.reshape(2, 4, 16, D)
        for n in range(2):
            f = i * 2 + n
            src, dst = done.at[f], out.at[:, rows16(frame), :]

            @pl.when(f != frame)
            def _():
                remote(src, dst, home_send, home_recv, (f, patch)).start()

            @pl.when(f == frame)
            def _():
                pltpu.make_async_copy(src, dst, home_recv).start()

        return 0

    lax.fori_loop(0, 4, finish, 0)
    pltpu.make_async_copy(full, full, gather_send).wait()
    pltpu.make_async_copy(tok_t.at[pl.ds(0, 7)], tok_t.at[pl.ds(0, 7)], tok_send).wait()
    pltpu.make_async_copy(att.at[pl.ds(0, 2032), :], att.at[pl.ds(0, 2032), :], att_send).wait()
    pltpu.make_async_copy(done.at[pl.ds(0, 7)], done.at[pl.ds(0, 7)], home_send).wait()
    pltpu.make_async_copy(out, out, home_recv).wait()


def shards(tokens, w_qkv_s, w_out_s, mod_s, w_qkv_t, w_out_t, mod_t):
    dma = pltpu.SemaphoreType.DMA
    return pl.pallas_call(
        fused_kernel,
        name="blocks",
        out_shape=jax.ShapeDtypeStruct((4, 128, D), BF),
        in_specs=[VMEM, VMEM, VMEM, ANY, ANY, ANY, ANY],
        out_specs=VMEM,
        scratch_shapes=[
            pltpu.VMEM((4, 128, D), BF),
            pltpu.VMEM((2, 128, D), BF),
            pltpu.VMEM((16, 128, D), BF),
            pltpu.VMEM((D, 3 * WIN), BF),
            pltpu.VMEM((ROWS, 2 * WIN), BF),
            pltpu.VMEM((4, 80, ROWS), BF),
            pltpu.VMEM((WIN, QT), F32),
            pltpu.VMEM((ROWS, QT), F32),
            pltpu.VMEM((ROWS, QT), F32),
            pltpu.VMEM((8, QT), F32),
            pltpu.VMEM((8, QT), F32),
            pltpu.VMEM((WIN, QT), F32),
            pltpu.VMEM((ROWS, WIN), BF),
            pltpu.VMEM((4, 32, 16, WIN), BF),
            pltpu.VMEM((8, 4, 16, D), BF),
            pltpu.VMEM((D, D), BF),
            pltpu.VMEM((D, 3 * D), BF),
            pltpu.VMEM((D, D), BF),
            pltpu.VMEM((512, D), BF),
            pltpu.VMEM((512, D), BF),
            pltpu.VMEM((512, D), BF),
            pltpu.VMEM((512, 3 * D), BF),
            pltpu.VMEM((512, D), BF),
            pltpu.VMEM((8, 4, 16, D), BF),
            dma((6,)),
            dma((2,)),
            dma((16,)),
            dma,
            dma,
            dma,
            dma,
            dma,
            dma,
            dma,
        ],
        compiler_params=params(1),
    )(tokens, mod_s, mod_t, w_qkv_s, w_out_s, w_qkv_t, w_out_t)


def solution(mesh):
    return jax.shard_map(
        shards,
        mesh=mesh,
        in_specs=(P("frame", "patch", None), P(), P(), P(), P(), P(), P()),
        out_specs=P("frame", "patch", None),
        check_vma=False,
    )
```

time: 396 us -> 120 us (0.30)
  the two profiles are of different devices: /device:TPU:32 before, /device:TPU:38 now
where the time goes in v2:
time: 120 us
  Pallas kernels  118 us (98%)
  local copies, waits for them, and re-layouts  2.37 us (2%)
    pallas_call x1, Pallas kernels, shards(): pl.pallas_call(fused_kernel, name='blocks', out_shape=jax.ShapeDtypeStruc...  118 us

profile of v2, /device:TPU:38, one launch (start us, length us, event | category | flops | bytes accessed | tf_op | source)
XLA Modules:
  0.0 120.3 jit_solution(1118863132289851308)
XLA Ops:
  0.0 117.9 %blocks.1 = bf16[4,128,1152]{2,1,0:T(8,128)(2,1)} custom-call(bf16[4,128,1152]{2,1,0:T(8,128)(2,1)} %tok.1, f32[3,1152]{1,0:T(4,128)} %mod_s.1, f32[3,1152]{1,0:T(4,128)} %mod_t.1, bf16[1152,3456]{1,0:T(8,128)(2,1)} %w_qkv_s.1, bf16[1152,1152]{1,0:T(8,128)(2,1)} %w_out_s.1, bf16[1152,3456]{1,0:T(8,128)(2,1)} %w_qkv_t.1, bf16[1152,1152]{1,0:T(8,128)(2,1)} %w_out_t.1), custom_call_target="tpu_custom_call" | custom-call | tf_op jit(solution)/shard_map/blocks/pallas_call | solution.py:318
  118.0 2.4 %copy.9 = bf16[4,128,1152]{2,1,0:T(8,128)(2,1)} copy(bf16[4,128,1152]{2,1,0:T(8,128)(2,1)} %blocks.1) | data formatting | bytes 2359296

commit v3 on v2

--- a/solution.py
+++ b/solution.py
@@ -96,7 +96,7 @@
     tok, mod_s, mod_t, w_qkv_s, w_out_s, w_qkv_t, w_out_t, out,
     hs, zbuf, full, wbuf, qk, vt, vwide, s0, s1, m0, m1, awide, att, att_t, tok_t, wo_s, wq, wo,
     flat, mid, hp, qkv, mixed_all, done,
-    w_sem, z_sem, full_sem, gather_send, tok_send, tok_recv, att_send, att_recv, home_send, home_recv,
+    w_sem, z_sem, full_sem, gather_send, tok_send, tok_recv, att_send, att_recv, home_send, home_recv, group_sem,
 ):
     frame, patch, zh, x, core = place()
     group = (x % 2) * 2 + core
@@ -107,12 +107,10 @@
 
     barrier = pltpu.get_barrier_semaphore()
 
-    def signal(i, _):
-        device = ((frame + i // 16) % 8, (patch + i % 16) % 16)
-        pl.semaphore_signal(barrier, inc=1, device_id=device, device_id_type=MESH)
-        return 0
-
-    lax.fori_loop(1, 128, signal, 0)
+    for d in range(1, 16):
+        pl.semaphore_signal(barrier, inc=1, device_id=(frame, (patch + d) % 16), device_id_type=MESH)
+    for d in range(1, 8):
+        pl.semaphore_signal(barrier, inc=1, device_id=((frame + d) % 8, patch), device_id_type=MESH)
     windows = load_window(w_qkv_s, wbuf, w_sem, group)
     loads = [
         pltpu.make_async_copy(src, dst, w_sem.at[3 + i])
@@ -126,9 +124,11 @@
 
     norm(2 * (1 - zh))
     norm(2 * (1 - zh) + 1)
-    pl.semaphore_wait(barrier, 127)
+    pl.semaphore_wait(barrier, 22)
     for j in range(2):
         remote(hs.at[2 * (1 - zh) + j], zbuf.at[j], gather_send, z_sem.at[j], zdev).start()
+    for d in range(1, 8):
+        pl.semaphore_signal(group_sem, inc=1, device_id=((frame + d) % 8, patch), device_id_type=MESH)
     norm(2 * zh)
     norm(2 * zh + 1)
 
@@ -162,6 +162,8 @@
         pltpu.make_async_copy(zbuf.at[j], zbuf.at[j], z_sem.at[j]).wait()
     along_x(lambda j: zbuf.at[j], zpatch)
 
+    lax.fori_loop(1, 8, chip, 0)
+
     def tokens_out(d, _):
         f = (frame + d) % 8
         remote(tok.at[:, rows16(f), :], tok_t.at[frame], tok_send, tok_recv, (f, patch)).start()
@@ -169,7 +171,7 @@
 
     lax.fori_loop(1, 8, tokens_out, 0)
     pltpu.make_async_copy(tok.at[:, rows16(frame), :], tok_t.at[frame], tok_recv).start()
-    lax.fori_loop(1, 8, chip, 0)
+    pl.semaphore_wait(group_sem, 7)
 
     scores, tops = (s0, s1), (m0, m1)
     first = patch // 2
@@ -356,6 +358,7 @@
             dma,
             dma,
             dma,
+            pltpu.SemaphoreType.REGULAR,
         ],
         compiler_params=params(1),
     )(tokens, mod_s, mod_t, w_qkv_s, w_out_s, w_qkv_t, w_out_t)

time: 120 us -> 120 us (level)
  the two profiles are of different devices: /device:TPU:38 before, /device:TPU:32 now
where the time goes in v3:
time: 120 us; the launch traced here: 119 us
  Pallas kernels  117 us (98%)
  local copies, waits for them, and re-layouts  2.37 us (2%)
    pallas_call x1, Pallas kernels, shards(): pl.pallas_call(fused_kernel, name='blocks', out_shape=jax.ShapeDtypeStruc...  117 us

profile of v3, /device:TPU:32, one launch (start us, length us, event | category | flops | bytes accessed | tf_op | source)
XLA Modules:
  0.0 119.5 jit_solution(15197134310861052520)
XLA Ops:
  0.0 117.1 %blocks.1 = bf16[4,128,1152]{2,1,0:T(8,128)(2,1)} custom-call(bf16[4,128,1152]{2,1,0:T(8,128)(2,1)} %tok.1, f32[3,1152]{1,0:T(4,128)} %mod_s.1, f32[3,1152]{1,0:T(4,128)} %mod_t.1, bf16[1152,3456]{1,0:T(8,128)(2,1)} %w_qkv_s.1, bf16[1152,1152]{1,0:T(8,128)(2,1)} %w_out_s.1, bf16[1152,3456]{1,0:T(8,128)(2,1)} %w_qkv_t.1, bf16[1152,1152]{1,0:T(8,128)(2,1)} %w_out_t.1), custom_call_target="tpu_custom_call" | custom-call | tf_op jit(solution)/shard_map/blocks/pallas_call | solution.py:320
  117.1 2.4 %copy.9 = bf16[4,128,1152]{2,1,0:T(8,128)(2,1)} copy(bf16[4,128,1152]{2,1,0:T(8,128)(2,1)} %blocks.1) | data formatting | bytes 2359296

commit v4 on v3

--- a/solution.py
+++ b/solution.py
@@ -84,19 +84,23 @@
     return copies
 
 
-def swap_rows(forward):
+def to_patches():
     row = lax.broadcasted_iota(jnp.int32, (512, 512), 0)
     col = lax.broadcasted_iota(jnp.int32, (512, 512), 1)
-    if forward:
-        return jnp.where(col == (row % 32) * 16 + row // 32, 1.0, 0.0).astype(BF)
-    return jnp.where(col == (row % 16) * 32 + row // 16, 1.0, 0.0).astype(BF)
+    return jnp.where(col == (row % 32) * 16 + row // 32, 1.0, 0.0).astype(BF)
+
+
+def to_frames():
+    row = lax.broadcasted_iota(jnp.int32, (256, 256), 0)
+    col = lax.broadcasted_iota(jnp.int32, (256, 256), 1)
+    return jnp.where(col == (row % 8) * 32 + row // 8, 1.0, 0.0).astype(BF)
 
 
 def fused_kernel(
-    tok, mod_s, mod_t, w_qkv_s, w_out_s, w_qkv_t, w_out_t, out,
-    hs, zbuf, full, wbuf, qk, vt, vwide, s0, s1, m0, m1, awide, att, att_t, tok_t, wo_s, wq, wo,
+    tok_hbm, mod_s, mod_t, w_qkv_s, w_out_s, w_qkv_t, w_out_t, out,
+    tok, hs, zbuf, full, wbuf, qk, vt, vwide, s0, s1, m0, m1, held, held_top, awide, att, att_t, tok_t, wo_s, wq, wo,
     flat, mid, hp, qkv, mixed_all, done,
-    w_sem, z_sem, full_sem, gather_send, tok_send, tok_recv, att_send, att_recv, home_send, home_recv, group_sem,
+    tok_sem, w_sem, z_sem, full_sem, gather_send, tok_send, tok_recv, att_send, att_recv, home_send, home_recv, group_sem,
 ):
     frame, patch, zh, x, core = place()
     group = (x % 2) * 2 + core
@@ -111,6 +115,8 @@
         pl.semaphore_signal(barrier, inc=1, device_id=(frame, (patch + d) % 16), device_id_type=MESH)
     for d in range(1, 8):
         pl.semaphore_signal(barrier, inc=1, device_id=((frame + d) % 8, patch), device_id_type=MESH)
+    load_tok = pltpu.make_async_copy(tok_hbm, tok, tok_sem)
+    load_tok.start()
     windows = load_window(w_qkv_s, wbuf, w_sem, group)
     loads = [
         pltpu.make_async_copy(src, dst, w_sem.at[3 + i])
@@ -122,6 +128,7 @@
     def norm(f):
         hs[f] = modulate(tok[f].astype(F32), mod_s)
 
+    load_tok.wait()
     norm(2 * (1 - zh))
     norm(2 * (1 - zh) + 1)
     pl.semaphore_wait(barrier, 22)
@@ -162,7 +169,7 @@
         pltpu.make_async_copy(zbuf.at[j], zbuf.at[j], z_sem.at[j]).wait()
     along_x(lambda j: zbuf.at[j], zpatch)
 
-    lax.fori_loop(1, 8, chip, 0)
+    lax.fori_loop(1, 5, chip, 0)
 
     def tokens_out(d, _):
         f = (frame + d) % 8
@@ -171,42 +178,36 @@
 
     lax.fori_loop(1, 8, tokens_out, 0)
     pltpu.make_async_copy(tok.at[:, rows16(frame), :], tok_t.at[frame], tok_recv).start()
-    pl.semaphore_wait(group_sem, 7)
 
     scores, tops = (s0, s1), (m0, m1)
-    first = patch // 2
-
-    def score(head, tile, slot):
+
+    def score(head, tile, slot, start, count):
         base = (head // 2) * 128
         rows = pl.ds(pl.multiple_of(tile * QT, QT), QT)
         keep = head_lanes((QT, 256), head, group)
         query = jnp.where(keep, qk[rows, base : base + 256], jnp.zeros((), BF))
         top = None
-        for c in range(ROWS // KC):
-            keys = qk[c * KC : (c + 1) * KC, WIN + base : WIN + base + 256]
+        for c in range(count):
+            keys = qk[pl.ds(pl.multiple_of(start + c * KC, KC), KC), WIN + base : WIN + base + 256]
             part = lax.dot_general(keys, query, (((1,), (1,)), ((), ())), preferred_element_type=F32)
             scores[slot][c * KC : (c + 1) * KC, :] = part
             part = jnp.max(part.reshape(KC // 8, 8, QT), axis=0)
             top = part if top is None else jnp.maximum(top, part)
         tops[slot][...] = jnp.broadcast_to(jnp.max(top, axis=0, keepdims=True), (8, QT))
 
-    def mix(head, slot):
-        top = tops[slot][0:1, :]
+    def sums(head, slot, start, count, top):
         acc = None
-        for c in range(ROWS // KC):
-            span = slice(c * KC, (c + 1) * KC)
-            probs = jnp.exp2(scores[slot][span, :] - top).astype(BF)
-            part = jnp.dot(vt[head, :, span], probs, preferred_element_type=F32)
+        for c in range(count):
+            probs = jnp.exp2(scores[slot][c * KC : (c + 1) * KC, :] - top).astype(BF)
+            values = vt[head, :, pl.ds(pl.multiple_of(start + c * KC, KC), KC)]
+            part = jnp.dot(values, probs, preferred_element_type=F32)
             acc = part if acc is None else acc + part
+        return acc
+
+    def keep_head(head, acc):
         awide[pl.ds(pl.multiple_of(32 * group + HD * head, 8), HD), :] = acc[:HD] / acc[HD : HD + 1]
 
-    score(0, first, 0)
-
-    def attend(i, _):
-        tile = (first + i) % 8
-        for head in range(4):
-            score((head + 1) % 4, tile if head < 3 else (first + i + 1) % 8, (head + 1) % 2)
-            mix(head, head % 2)
+    def send_tile(tile):
         att[pl.ds(pl.multiple_of(tile * QT, QT), QT), :] = awide[...].T.astype(BF)
 
         def go(n, _):
@@ -225,9 +226,50 @@
             return 0
 
         lax.fori_loop(0, 16, go, 0)
-        return 0
-
-    lax.fori_loop(0, 8, attend, 0)
+
+    half = ROWS // 2
+    near, far = zh * half, (1 - zh) * half
+    score(0, zh * 4 + x, 0, near, 4)
+
+    def first_part(i, _):
+        for head in range(4):
+            ahead = (x + i) % 4 if head < 3 else (x + i + 1) % 4
+            score((head + 1) % 4, zh * 4 + ahead, (head + 1) % 2, near, 4)
+            slot = head % 2
+            held[(x + i) % 4, head] = sums(head, slot, near, 4, tops[slot][0:1, :])
+            held_top[(x + i) % 4, head] = tops[slot][...]
+        return 0
+
+    lax.fori_loop(0, 4, first_part, 0)
+    lax.fori_loop(5, 8, chip, 0)
+    pl.semaphore_wait(group_sem, 7)
+    score(0, zh * 4 + x, 0, far, 4)
+
+    def second_part(i, _):
+        for head in range(4):
+            ahead = (x + i) % 4 if head < 3 else (x + i + 1) % 4
+            score((head + 1) % 4, zh * 4 + ahead, (head + 1) % 2, far, 4)
+            slot = head % 2
+            before = held_top[(x + i) % 4, head, 0:1, :]
+            top = jnp.maximum(tops[slot][0:1, :], before)
+            acc = held[(x + i) % 4, head] * jnp.exp2(before - top)
+            keep_head(head, acc + sums(head, slot, far, 4, top))
+        send_tile(zh * 4 + (x + i) % 4)
+        return 0
+
+    lax.fori_loop(0, 4, second_part, 0)
+    score(0, (1 - zh) * 4 + x, 0, 0, 8)
+
+    def other_tiles(i, _):
+        for head in range(4):
+            ahead = (x + i) % 4 if head < 3 else (x + i + 1) % 4
+            score((head + 1) % 4, (1 - zh) * 4 + ahead, (head + 1) % 2, 0, 8)
+            slot = head % 2
+            keep_head(head, sums(head, slot, 0, 8, tops[slot][0:1, :]))
+        send_tile((1 - zh) * 4 + (x + i) % 4)
+        return 0
+
+    lax.fori_loop(0, 4, other_tiles, 0)
 
     for load in loads:
         load.wait()
@@ -246,18 +288,12 @@
         proj = jnp.dot(flat[rows, :], wo_s[...], preferred_element_type=F32)
         values = tok_t[pl.ds(i * 4, 4)].reshape(256, D).astype(F32)
         values = (values + mod_s[2:3, :] * proj).astype(BF)
-        mid[rows, :] = values
+        mid[pl.ds(i * 16, 16)] = values.astype(F32).reshape(16, 16, D)
         flat[rows, :] = modulate(values.astype(F32), mod_t)
         return 0
 
     lax.fori_loop(0, 2, finish_mid, 0)
-    hp[...] = jnp.dot(swap_rows(True), flat[...], preferred_element_type=F32).astype(BF)
-    for part in range(9):
-        cols = slice(part * WIN, (part + 1) * WIN)
-        acc = jnp.dot(hp[...], wq[:, cols], preferred_element_type=F32)
-        if part < 3:
-            acc = acc * SCALE
-        qkv[:, cols] = acc.astype(BF)
+    hp[...] = jnp.dot(to_patches(), flat[...], preferred_element_type=F32).astype(BF)
 
     row = lax.broadcasted_iota(jnp.int32, (128, 128), 0)
     col = lax.broadcasted_iota(jnp.int32, (128, 128), 1)
@@ -266,8 +302,10 @@
 
     def four_patches(i, _):
         rows = pl.ds(pl.multiple_of(i * 128, 128), 128)
+        tiles = [None] * 9
         for head in range(HEADS):
-            base = min(head * HD // 128, 7) * 128
+            tile = min(head * HD // 128, 7)
+            base = tile * 128
             low = head * HD - base
             keep = (lane >= low) & (lane < low + HD)
             query = jnp.where(keep, qkv[rows, base : base + 256], jnp.zeros((), BF))
@@ -277,53 +315,57 @@
             expo = jnp.exp2(part - jnp.max(part, axis=-1, keepdims=True))
             probs = (expo / jnp.sum(expo, axis=-1, keepdims=True)).astype(BF)
             mixed = jnp.dot(probs, qkv[rows, 2 * D + base : 2 * D + base + 256], preferred_element_type=F32)
-            mixed = mixed.astype(BF)
-            if low == 0:
-                mixed_all[rows, base : base + 256] = mixed
-            else:
-                mixed_all[rows, base : base + 256] = jnp.where(keep, mixed, mixed_all[rows, base : base + 256])
-        return 0
-
-    lax.fori_loop(0, 4, four_patches, 0)
-    flat[...] = jnp.dot(swap_rows(False), mixed_all[...], preferred_element_type=F32).astype(BF)
-
-    def finish(i, _):
-        i = (frame // 2 + i) % 4
-        rows = pl.ds(pl.multiple_of(i * 128, 128), 128)
-        proj = jnp.dot(flat[rows, :], wo[...], preferred_element_type=F32)
-        values = (mid[rows, :].astype(F32) + mod_t[2:3, :] * proj).astype(BF)
-        done[pl.ds(i * 2, 2)] = values.reshape(2, 4, 16, D)
-        for n in range(2):
-            f = i * 2 + n
-            src, dst = done.at[f], out.at[:, rows16(frame), :]
-
-            @pl.when(f != frame)
-            def _():
-                remote(src, dst, home_send, home_recv, (f, patch)).start()
-
-            @pl.when(f == frame)
-            def _():
-                pltpu.make_async_copy(src, dst, home_recv).start()
-
-        return 0
-
-    lax.fori_loop(0, 4, finish, 0)
+            for n in range(2):
+                piece = mixed[:, n * 128 : n * 128 + 128]
+                old = tiles[tile + n]
+                tiles[tile + n] = piece if old is None else jnp.where(keep[:, n * 128 : n * 128 + 128], piece, old)
+        for n in range(9):
+            mixed_all[rows, n * 128 : n * 128 + 128] = tiles[n].astype(BF)
+        return 0
+
+    def eight_patches(n, _):
+        rows = pl.ds(pl.multiple_of(n * 256, 256), 256)
+        for part in range(9):
+            cols = slice(part * WIN, (part + 1) * WIN)
+            acc = jnp.dot(hp[rows, :], wq[:, cols], preferred_element_type=F32)
+            if part < 3:
+                acc = acc * SCALE
+            qkv[:, cols] = acc.astype(BF)
+        lax.fori_loop(0, 2, four_patches, 0)
+        ordered = jnp.dot(to_frames(), mixed_all[...], preferred_element_type=F32).astype(BF)
+        proj = jnp.dot(ordered, wo[...], preferred_element_type=F32)
+        values = mid[:, pl.ds(pl.multiple_of(n * 8, 8), 8), :].reshape(256, D)
+        values = (values + mod_t[2:3, :] * proj).astype(BF)
+        done[n] = values.reshape(8, 32, D)
+
+        def go(d, _):
+            f = (frame + d) % 8
+            remote(done.at[n, f], out.at[n, frame], home_send, home_recv, (f, patch)).start()
+            return 0
+
+        lax.fori_loop(1, 8, go, 0)
+        pltpu.make_async_copy(done.at[n, frame], out.at[n, frame], home_recv).start()
+        return 0
+
+    lax.fori_loop(0, 2, eight_patches, 0)
     pltpu.make_async_copy(full, full, gather_send).wait()
     pltpu.make_async_copy(tok_t.at[pl.ds(0, 7)], tok_t.at[pl.ds(0, 7)], tok_send).wait()
     pltpu.make_async_copy(att.at[pl.ds(0, 2032), :], att.at[pl.ds(0, 2032), :], att_send).wait()
-    pltpu.make_async_copy(done.at[pl.ds(0, 7)], done.at[pl.ds(0, 7)], home_send).wait()
+    for n in range(2):
+        pltpu.make_async_copy(done.at[n, pl.ds(0, 7)], done.at[n, pl.ds(0, 7)], home_send).wait()
     pltpu.make_async_copy(out, out, home_recv).wait()
 
 
 def shards(tokens, w_qkv_s, w_out_s, mod_s, w_qkv_t, w_out_t, mod_t):
     dma = pltpu.SemaphoreType.DMA
-    return pl.pallas_call(
+    parts = pl.pallas_call(
         fused_kernel,
         name="blocks",
-        out_shape=jax.ShapeDtypeStruct((4, 128, D), BF),
-        in_specs=[VMEM, VMEM, VMEM, ANY, ANY, ANY, ANY],
-        out_specs=VMEM,
+        out_shape=jax.ShapeDtypeStruct((2, 8, 32, D), BF),
+        in_specs=[ANY, VMEM, VMEM, ANY, ANY, ANY, ANY],
+        out_specs=ANY,
         scratch_shapes=[
+            pltpu.VMEM((4, 128, D), BF),
             pltpu.VMEM((4, 128, D), BF),
             pltpu.VMEM((2, 128, D), BF),
             pltpu.VMEM((16, 128, D), BF),
@@ -335,6 +377,8 @@
             pltpu.VMEM((ROWS, QT), F32),
             pltpu.VMEM((8, QT), F32),
             pltpu.VMEM((8, QT), F32),
+            pltpu.VMEM((4, 4, 80, QT), F32),
+            pltpu.VMEM((4, 4, 8, QT), F32),
             pltpu.VMEM((WIN, QT), F32),
             pltpu.VMEM((ROWS, WIN), BF),
             pltpu.VMEM((4, 32, 16, WIN), BF),
@@ -343,11 +387,12 @@
             pltpu.VMEM((D, 3 * D), BF),
             pltpu.VMEM((D, D), BF),
             pltpu.VMEM((512, D), BF),
+            pltpu.VMEM((32, 16, D), F32),
             pltpu.VMEM((512, D), BF),
-            pltpu.VMEM((512, D), BF),
-            pltpu.VMEM((512, 3 * D), BF),
-            pltpu.VMEM((512, D), BF),
-            pltpu.VMEM((8, 4, 16, D), BF),
+            pltpu.VMEM((256, 3 * D), BF),
+            pltpu.VMEM((256, D), BF),
+            pltpu.VMEM((2, 8, 32, D), BF),
+            dma,
             dma((6,)),
             dma((2,)),
             dma((16,)),
@@ -362,6 +407,7 @@
         ],
         compiler_params=params(1),
     )(tokens, mod_s, mod_t, w_qkv_s, w_out_s, w_qkv_t, w_out_t)
+    return parts.reshape(2, 8, 4, 8, D).transpose(2, 1, 0, 3, 4).reshape(4, 128, D)
 
 
 def solution(mesh):

time: 120 us -> 112 us (0.933)
  Pallas kernels: 117 us -> 109 us
    pallas_call x1, Pallas kernels: 117 us -> 109 us  [shards(): pl.pallas_call(fused_kernel, name='blocks', out_shape=jax.ShapeDtypeStruc...]
    transpose x0 -> x1, local copies, waits for them, and re-layouts: none -> 2.37 us  [shards(): parts.reshape(2, 8, 4, 8, D).transpose(2, 1, 0, 3, 4).reshape(4, 128, D)]
    unnamed x1 -> x0, local copies, waits for them, and re-layouts: 2.37 us -> none
where the time goes in v4:
time: 112 us; the launch traced here: 111 us
  Pallas kernels  109 us (97%)
  local copies, waits for them, and re-layouts  2.37 us (2%)
    pallas_call x1, Pallas kernels, shards(): pl.pallas_call(fused_kernel, name='blocks', out_shape=jax.ShapeDtypeStruc...  109 us
    transpose x1, local copies, waits for them, and re-layouts, shards(): parts.reshape(2, 8, 4, 8, D).transpose(2, 1, 0, 3, 4).reshape(4, 128, D)  2.37 us

profile of v4, /device:TPU:32, one launch (start us, length us, event | category | flops | bytes accessed | tf_op | source)
XLA Modules:
  0.0 111.4 jit_solution(7447732830947356086)
XLA Ops:
  0.0 109.1 %blocks.1 = bf16[2,8,32,1152]{3,2,1,0:T(8,128)(2,1)} custom-call(bf16[4,128,1152]{2,1,0:T(8,128)(2,1)} %tok_hbm.1, f32[3,1152]{1,0:T(4,128)} %mod_s.1, f32[3,1152]{1,0:T(4,128)} %mod_t.1, bf16[1152,3456]{1,0:T(8,128)(2,1)} %w_qkv_s.1, bf16[1152,1152]{1,0:T(8,128)(2,1)} %w_out_s.1, bf16[1152,3456]{1,0:T(8,128)(2,1)} %w_qkv_t.1, bf16[1152,1152]{1,0:T(8,128)(2,1)} %w_out_t.1), custom_call_target="tpu_custom_call" | custom-call | tf_op jit(solution)/shard_map/blocks/pallas_call | solution.py:361
  109.1 2.4 %copy.8 = bf16[4,8,2,8,1152]{4,3,2,1,0:T(8,128)(2,1)} copy(bf16[4,8,2,8,1152]{4,3,0,1,2:T(8,128)(2,1)} %bitcast.4) | data formatting | bytes 2359296 | tf_op jit(solution)/shard_map/transpose | solution.py:410

commit v5 on v4

--- a/solution.py
+++ b/solution.py
@@ -52,26 +52,39 @@
     return pl.ds(pl.multiple_of(index * 16, 16), 16)
 
 
-def head_lanes(shape, head, group):
+def head_lanes(shape, head):
     lane = lax.broadcasted_iota(jnp.int32, shape, 1) + (head // 2) * 128
-    low = 32 * group + HD * head
-    return (lane >= low) & (lane < low + HD)
-
-
-def project(h, w, qk, vt, vwide, index, group):
+    return (lane >= HD * head) & (lane < HD * head + HD)
+
+
+def pack_weights(wbuf, packed, group):
+    row = lax.broadcasted_iota(jnp.int32, (2 * WIN, 640), 0)
+    col = lax.broadcasted_iota(jnp.int32, (2 * WIN, 640), 1)
+    width = 4 * HD
+    target = jnp.where(col < width, col, col + (WIN - width)) + 32 * group
+    pick = jnp.where((row == target) & (col < 2 * width), 1.0, 0.0).astype(BF)
+    row = lax.broadcasted_iota(jnp.int32, (WIN, WIN), 0)
+    col = lax.broadcasted_iota(jnp.int32, (WIN, WIN), 1)
+    first = jnp.where((row == col + 32 * group) & (col < width), 1.0, 0.0).astype(BF)
+
+    def some(i, _):
+        rows = pl.ds(pl.multiple_of(i * 384, 384), 384)
+        packed[rows, :WIN] = jnp.dot(wbuf[rows, :WIN], first, preferred_element_type=F32).astype(BF)
+        packed[rows, WIN:] = jnp.dot(wbuf[rows, WIN:], pick, preferred_element_type=F32).astype(BF)
+        return 0
+
+    lax.fori_loop(0, 3, some, 0)
+
+
+def project(h, packed, qk, vt, index):
     rows = pl.ds(pl.multiple_of(index * QT, QT), QT)
-    for part in range(3):
-        cols = slice(part * WIN, (part + 1) * WIN)
-        acc = jnp.dot(h, w[:, cols], preferred_element_type=F32)
-        if part == 0:
-            acc = acc * SCALE
-        if part < 2:
-            qk[rows, cols] = acc.astype(BF)
-        else:
-            vwide[...] = acc.T
+    acc = jnp.dot(h, packed[...], preferred_element_type=F32)
+    qk[rows, :WIN] = (acc[:, :WIN] * SCALE).astype(BF)
+    qk[rows, WIN:] = acc[:, WIN : 2 * WIN].astype(BF)
+    values = acc[:, 640:1024].T
     one = jnp.where(lax.broadcasted_iota(jnp.int32, (8, QT), 0) == 0, 1.0, 0.0)
     for head in range(4):
-        part = vwide[pl.ds(pl.multiple_of(32 * group + HD * head, 8), HD), :]
+        part = values[32 + HD * head : 32 + HD * head + HD, :]
         vt[head, :, rows] = jnp.concatenate([part, one], axis=0).astype(BF)
 
 
@@ -98,7 +111,7 @@
 
 def fused_kernel(
     tok_hbm, mod_s, mod_t, w_qkv_s, w_out_s, w_qkv_t, w_out_t, out,
-    tok, hs, zbuf, full, wbuf, qk, vt, vwide, s0, s1, m0, m1, held, held_top, awide, att, att_t, tok_t, wo_s, wq, wo,
+    tok, hs, zbuf, full, wbuf, packed, qk, vt, s0, s1, m0, m1, held, held_top, awide, att, att_t, tok_t, wo_s, wq, wo,
     flat, mid, hp, qkv, mixed_all, done,
     tok_sem, w_sem, z_sem, full_sem, gather_send, tok_send, tok_recv, att_send, att_recv, home_send, home_recv, group_sem,
 ):
@@ -140,7 +153,7 @@
     norm(2 * zh + 1)
 
     def along_x(chunk, source):
-        for d in (1, 3, 2):
+        for d in (2, 1, 3):
             xd = (x + d) % 4
             remote(chunk(xd // 2), full.at[source], gather_send, full_sem.at[source], (frame, zh * 8 + xd * 2 + core)).start()
         pltpu.make_async_copy(chunk(x // 2), full.at[source], full_sem.at[source]).start()
@@ -149,25 +162,37 @@
     awide[...] = jnp.zeros_like(awide)
     for window in windows:
         window.wait()
+    pack_weights(wbuf, packed, group)
 
     def arrived(source):
         pltpu.make_async_copy(full.at[source], full.at[source], full_sem.at[source]).wait()
 
     def chip(k, _):
         plane = (zh + k // 4) % 2
-        index = plane * 4 + (x + k % 4) % 4
+        step = 2 * (k % 4) - 3 * (k % 4 // 2)
+        index = plane * 4 + (x + step) % 4
         source = index * 2 + core
         arrived(source)
         remote(full.at[source], full.at[source], gather_send, full_sem.at[source], sibling).start()
         arrived(index * 2 + 1 - core)
         h = full[pl.ds(index * 2, 2)].reshape(QT, D)
-        project(h, wbuf, qk, vt, vwide, index, group)
+        project(h, packed, qk, vt, index)
         return 0
 
     chip(0, 0)
     for j in range(2):
         pltpu.make_async_copy(zbuf.at[j], zbuf.at[j], z_sem.at[j]).wait()
-    along_x(lambda j: zbuf.at[j], zpatch)
+        for n in range(2):
+            xd = 2 * j + n
+            src, dst = zbuf.at[j], full.at[zpatch]
+
+            @pl.when(xd != x)
+            def _():
+                remote(src, dst, gather_send, full_sem.at[zpatch], (frame, zh * 8 + xd * 2 + core)).start()
+
+            @pl.when(xd == x)
+            def _():
+                pltpu.make_async_copy(src, dst, full_sem.at[zpatch]).start()
 
     lax.fori_loop(1, 5, chip, 0)
 
@@ -181,25 +206,25 @@
 
     scores, tops = (s0, s1), (m0, m1)
 
-    def score(head, tile, slot, start, count):
+    def score(head, tile, slot, chunks):
         base = (head // 2) * 128
         rows = pl.ds(pl.multiple_of(tile * QT, QT), QT)
-        keep = head_lanes((QT, 256), head, group)
+        keep = head_lanes((QT, 256), head)
         query = jnp.where(keep, qk[rows, base : base + 256], jnp.zeros((), BF))
         top = None
-        for c in range(count):
-            keys = qk[pl.ds(pl.multiple_of(start + c * KC, KC), KC), WIN + base : WIN + base + 256]
+        for c, at_chunk in enumerate(chunks):
+            keys = qk[pl.ds(pl.multiple_of(at_chunk * KC, KC), KC), WIN + base : WIN + base + 256]
             part = lax.dot_general(keys, query, (((1,), (1,)), ((), ())), preferred_element_type=F32)
             scores[slot][c * KC : (c + 1) * KC, :] = part
             part = jnp.max(part.reshape(KC // 8, 8, QT), axis=0)
             top = part if top is None else jnp.maximum(top, part)
         tops[slot][...] = jnp.broadcast_to(jnp.max(top, axis=0, keepdims=True), (8, QT))
 
-    def sums(head, slot, start, count, top):
+    def sums(head, slot, chunks, top):
         acc = None
-        for c in range(count):
+        for c, at_chunk in enumerate(chunks):
             probs = jnp.exp2(scores[slot][c * KC : (c + 1) * KC, :] - top).astype(BF)
-            values = vt[head, :, pl.ds(pl.multiple_of(start + c * KC, KC), KC)]
+            values = vt[head, :, pl.ds(pl.multiple_of(at_chunk * KC, KC), KC)]
             part = jnp.dot(values, probs, preferred_element_type=F32)
             acc = part if acc is None else acc + part
         return acc
@@ -227,45 +252,45 @@
 
         lax.fori_loop(0, 16, go, 0)
 
-    half = ROWS // 2
-    near, far = zh * half, (1 - zh) * half
-    score(0, zh * 4 + x, 0, near, 4)
+    near = [zh * 4 + c for c in range(4)] + [(1 - zh) * 4 + x]
+    far = [(1 - zh) * 4 + (x + d) % 4 for d in (2, 1, 3)]
+    score(0, zh * 4 + x, 0, near)
 
     def first_part(i, _):
         for head in range(4):
             ahead = (x + i) % 4 if head < 3 else (x + i + 1) % 4
-            score((head + 1) % 4, zh * 4 + ahead, (head + 1) % 2, near, 4)
+            score((head + 1) % 4, zh * 4 + ahead, (head + 1) % 2, near)
             slot = head % 2
-            held[(x + i) % 4, head] = sums(head, slot, near, 4, tops[slot][0:1, :])
+            held[(x + i) % 4, head] = sums(head, slot, near, tops[slot][0:1, :])
             held_top[(x + i) % 4, head] = tops[slot][...]
         return 0
 
     lax.fori_loop(0, 4, first_part, 0)
     lax.fori_loop(5, 8, chip, 0)
     pl.semaphore_wait(group_sem, 7)
-    score(0, zh * 4 + x, 0, far, 4)
+    score(0, zh * 4 + x, 0, far)
 
     def second_part(i, _):
         for head in range(4):
             ahead = (x + i) % 4 if head < 3 else (x + i + 1) % 4
-            score((head + 1) % 4, zh * 4 + ahead, (head + 1) % 2, far, 4)
+            score((head + 1) % 4, zh * 4 + ahead, (head + 1) % 2, far)
             slot = head % 2
             before = held_top[(x + i) % 4, head, 0:1, :]
             top = jnp.maximum(tops[slot][0:1, :], before)
             acc = held[(x + i) % 4, head] * jnp.exp2(before - top)
-            keep_head(head, acc + sums(head, slot, far, 4, top))
+            keep_head(head, acc + sums(head, slot, far, top))
         send_tile(zh * 4 + (x + i) % 4)
         return 0
 
     lax.fori_loop(0, 4, second_part, 0)
-    score(0, (1 - zh) * 4 + x, 0, 0, 8)
+    score(0, (1 - zh) * 4 + x, 0, range(8))
 
     def other_tiles(i, _):
         for head in range(4):
             ahead = (x + i) % 4 if head < 3 else (x + i + 1) % 4
-            score((head + 1) % 4, (1 - zh) * 4 + ahead, (head + 1) % 2, 0, 8)
+            score((head + 1) % 4, (1 - zh) * 4 + ahead, (head + 1) % 2, range(8))
             slot = head % 2
-            keep_head(head, sums(head, slot, 0, 8, tops[slot][0:1, :]))
+            keep_head(head, sums(head, slot, range(8), tops[slot][0:1, :]))
         send_tile((1 - zh) * 4 + (x + i) % 4)
         return 0
 
@@ -325,10 +350,9 @@
 
     def eight_patches(n, _):
         rows = pl.ds(pl.multiple_of(n * 256, 256), 256)
-        for part in range(9):
-            cols = slice(part * WIN, (part + 1) * WIN)
+        for cols in (slice(0, 768), slice(768, 1152), slice(1152, 1920), slice(1920, 2688), slice(2688, 3456)):
             acc = jnp.dot(hp[rows, :], wq[:, cols], preferred_element_type=F32)
-            if part < 3:
+            if cols.stop <= D:
                 acc = acc * SCALE
             qkv[:, cols] = acc.astype(BF)
         lax.fori_loop(0, 2, four_patches, 0)
@@ -370,9 +394,9 @@
             pltpu.VMEM((2, 128, D), BF),
             pltpu.VMEM((16, 128, D), BF),
             pltpu.VMEM((D, 3 * WIN), BF),
+            pltpu.VMEM((D, 1024), BF),
             pltpu.VMEM((ROWS, 2 * WIN), BF),
             pltpu.VMEM((4, 80, ROWS), BF),
-            pltpu.VMEM((WIN, QT), F32),
             pltpu.VMEM((ROWS, QT), F32),
             pltpu.VMEM((ROWS, QT), F32),
             pltpu.VMEM((8, QT), F32),

time: 112 us -> 109 us (0.973); the launches traced: 111 us -> 107 us
  Pallas kernels: 109 us -> 105 us
    pallas_call x1, Pallas kernels: 109 us -> 105 us  [shards(): pl.pallas_call(fused_kernel, name='blocks', out_shape=jax.ShapeDtypeStruc...]
where the time goes in v5:
time: 109 us; the launch traced here: 107 us
  Pallas kernels  105 us (96%)
  local copies, waits for them, and re-layouts  2.37 us (2%)
    pallas_call x1, Pallas kernels, shards(): pl.pallas_call(fused_kernel, name='blocks', out_shape=jax.ShapeDtypeStruc...  105 us
    transpose x1, local copies, waits for them, and re-layouts, shards(): parts.reshape(2, 8, 4, 8, D).transpose(2, 1, 0, 3, 4).reshape(4, 128, D)  2.37 us

profile of v5, /device:TPU:32, one launch (start us, length us, event | category | flops | bytes accessed | tf_op | source)
XLA Modules:
  0.0 107.2 jit_solution(16381497596740439531)
XLA Ops:
  0.0 104.8 %blocks.1 = bf16[2,8,32,1152]{3,2,1,0:T(8,128)(2,1)} custom-call(bf16[4,128,1152]{2,1,0:T(8,128)(2,1)} %tok_hbm.1, f32[3,1152]{1,0:T(4,128)} %mod_s.1, f32[3,1152]{1,0:T(4,128)} %mod_t.1, bf16[1152,3456]{1,0:T(8,128)(2,1)} %w_qkv_s.1, bf16[1152,1152]{1,0:T(8,128)(2,1)} %w_out_s.1, bf16[1152,3456]{1,0:T(8,128)(2,1)} %w_qkv_t.1, bf16[1152,1152]{1,0:T(8,128)(2,1)} %w_out_t.1), custom_call_target="tpu_custom_call" | custom-call | tf_op jit(solution)/shard_map/blocks/pallas_call | solution.py:385
  104.8 2.4 %copy.8 = bf16[4,8,2,8,1152]{4,3,2,1,0:T(8,128)(2,1)} copy(bf16[4,8,2,8,1152]{4,3,0,1,2:T(8,128)(2,1)} %bitcast.4) | data formatting | bytes 2359296 | tf_op jit(solution)/shard_map/transpose | solution.py:434

commit v6 on v5

--- a/solution.py
+++ b/solution.py
@@ -167,18 +167,29 @@
     def arrived(source):
         pltpu.make_async_copy(full.at[source], full.at[source], full_sem.at[source]).wait()
 
-    def chip(k, _):
-        plane = (zh + k // 4) % 2
-        step = 2 * (k % 4) - 3 * (k % 4 // 2)
-        index = plane * 4 + (x + step) % 4
-        source = index * 2 + core
+    def chip_of(k):
+        return ((zh + k // 4) % 2) * 4 + (x + 2 * (k % 4) - 3 * (k % 4 // 2)) % 4
+
+    def relay(k, _):
+        source = chip_of(k) * 2 + core
         arrived(source)
         remote(full.at[source], full.at[source], gather_send, full_sem.at[source], sibling).start()
+        return 0
+
+    def chip(k, _):
+        index = chip_of(k)
         arrived(index * 2 + 1 - core)
         h = full[pl.ds(index * 2, 2)].reshape(QT, D)
         project(h, packed, qk, vt, index)
         return 0
 
+    def token_out(f):
+        remote(tok.at[:, rows16(f), :], tok_t.at[frame], tok_send, tok_recv, (f, patch)).start()
+
+    for d in (2, 4, 6):
+        token_out((frame + d) % 8)
+    pltpu.make_async_copy(tok.at[:, rows16(frame), :], tok_t.at[frame], tok_recv).start()
+    relay(0, 0)
     chip(0, 0)
     for j in range(2):
         pltpu.make_async_copy(zbuf.at[j], zbuf.at[j], z_sem.at[j]).wait()
@@ -194,15 +205,11 @@
             def _():
                 pltpu.make_async_copy(src, dst, full_sem.at[zpatch]).start()
 
+    lax.fori_loop(1, 5, relay, 0)
+    for d in (1, 3, 5, 7):
+        token_out((frame + d) % 8)
     lax.fori_loop(1, 5, chip, 0)
 
-    def tokens_out(d, _):
-        f = (frame + d) % 8
-        remote(tok.at[:, rows16(f), :], tok_t.at[frame], tok_send, tok_recv, (f, patch)).start()
-        return 0
-
-    lax.fori_loop(1, 8, tokens_out, 0)
-    pltpu.make_async_copy(tok.at[:, rows16(frame), :], tok_t.at[frame], tok_recv).start()
 
     scores, tops = (s0, s1), (m0, m1)
 
@@ -236,7 +243,7 @@
         att[pl.ds(pl.multiple_of(tile * QT, QT), QT), :] = awide[...].T.astype(BF)
 
         def go(n, _):
-            f, p = n // 2, tile * 2 + n % 2
+            f, p = (frame + n // 2) % 8, tile * 2 + n % 2
             src, dst = att.at[rows16(p * 8 + f), :], att_t.at[group, at]
             mine = (f == frame) & (p == patch)
 
@@ -266,8 +273,21 @@
         return 0
 
     lax.fori_loop(0, 4, first_part, 0)
+    lax.fori_loop(5, 8, relay, 0)
     lax.fori_loop(5, 8, chip, 0)
     pl.semaphore_wait(group_sem, 7)
+    score(0, (1 - zh) * 4 + x, 0, range(8))
+
+    def other_tiles(i, _):
+        for head in range(4):
+            ahead = (x + i) % 4 if head < 3 else (x + i + 1) % 4
+            score((head + 1) % 4, (1 - zh) * 4 + ahead, (head + 1) % 2, range(8))
+            slot = head % 2
+            keep_head(head, sums(head, slot, range(8), tops[slot][0:1, :]))
+        send_tile((1 - zh) * 4 + (x + i) % 4)
+        return 0
+
+    lax.fori_loop(0, 4, other_tiles, 0)
     score(0, zh * 4 + x, 0, far)
 
     def second_part(i, _):
@@ -283,18 +303,6 @@
         return 0
 
     lax.fori_loop(0, 4, second_part, 0)
-    score(0, (1 - zh) * 4 + x, 0, range(8))
-
-    def other_tiles(i, _):
-        for head in range(4):
-            ahead = (x + i) % 4 if head < 3 else (x + i + 1) % 4
-            score((head + 1) % 4, (1 - zh) * 4 + ahead, (head + 1) % 2, range(8))
-            slot = head % 2
-            keep_head(head, sums(head, slot, range(8), tops[slot][0:1, :]))
-        send_tile((1 - zh) * 4 + (x + i) % 4)
-        return 0
-
-    lax.fori_loop(0, 4, other_tiles, 0)
 
     for load in loads:
         load.wait()

time: 109 us -> 101 us (0.927)
  Pallas kernels: 105 us -> 97.3 us
    pallas_call x1, Pallas kernels: 105 us -> 97.3 us  [shards(): pl.pallas_call(fused_kernel, name='blocks', out_shape=jax.ShapeDtypeStruc...]
where the time goes in v6:
time: 101 us; the launch traced here: 99.7 us
  Pallas kernels  97.3 us (96%)
  local copies, waits for them, and re-layouts  2.37 us (2%)
    pallas_call x1, Pallas kernels, shards(): pl.pallas_call(fused_kernel, name='blocks', out_shape=jax.ShapeDtypeStruc...  97.3 us
    transpose x1, local copies, waits for them, and re-layouts, shards(): parts.reshape(2, 8, 4, 8, D).transpose(2, 1, 0, 3, 4).reshape(4, 128, D)  2.37 us

profile of v6, /device:TPU:32, one launch (start us, length us, event | category | flops | bytes accessed | tf_op | source)
XLA Modules:
  0.0 99.7 jit_solution(12789748149117803714)
XLA Ops:
  0.0 97.3 %blocks.1 = bf16[2,8,32,1152]{3,2,1,0:T(8,128)(2,1)} custom-call(bf16[4,128,1152]{2,1,0:T(8,128)(2,1)} %tok_hbm.1, f32[3,1152]{1,0:T(4,128)} %mod_s.1, f32[3,1152]{1,0:T(4,128)} %mod_t.1, bf16[1152,3456]{1,0:T(8,128)(2,1)} %w_qkv_s.1, bf16[1152,1152]{1,0:T(8,128)(2,1)} %w_out_s.1, bf16[1152,3456]{1,0:T(8,128)(2,1)} %w_qkv_t.1, bf16[1152,1152]{1,0:T(8,128)(2,1)} %w_out_t.1), custom_call_target="tpu_custom_call" | custom-call | tf_op jit(solution)/shard_map/blocks/pallas_call | solution.py:393
  97.3 2.4 %copy.8 = bf16[4,8,2,8,1152]{4,3,2,1,0:T(8,128)(2,1)} copy(bf16[4,8,2,8,1152]{4,3,0,1,2:T(8,128)(2,1)} %bitcast.4) | data formatting | bytes 2359296 | tf_op jit(solution)/shard_map/transpose | solution.py:442

commit v7 on v6

--- a/solution.py
+++ b/solution.py
@@ -239,25 +239,20 @@
     def keep_head(head, acc):
         awide[pl.ds(pl.multiple_of(32 * group + HD * head, 8), HD), :] = acc[:HD] / acc[HD : HD + 1]
 
-    def send_tile(tile):
+    def store_tile(tile):
         att[pl.ds(pl.multiple_of(tile * QT, QT), QT), :] = awide[...].T.astype(BF)
 
-        def go(n, _):
-            f, p = (frame + n // 2) % 8, tile * 2 + n % 2
+    def send_quarter(tile, quarter, own=False):
+        for n in range(4):
+            d = quarter * 2 + n // 2
+            f, p = (frame + d) % 8, tile * 2 + n % 2
+            if own:
+                p = patch if n % 2 == 0 else sibling[1]
             src, dst = att.at[rows16(p * 8 + f), :], att_t.at[group, at]
-            mine = (f == frame) & (p == patch)
-
-            @pl.when(jnp.logical_not(mine))
-            def _():
+            if own and d == 0 and n % 2 == 0:
+                pltpu.make_async_copy(src, dst, att_recv).start()
+            else:
                 remote(src, dst, att_send, att_recv, (f, p)).start()
-
-            @pl.when(mine)
-            def _():
-                pltpu.make_async_copy(src, dst, att_recv).start()
-
-            return 0
-
-        lax.fori_loop(0, 16, go, 0)
 
     near = [zh * 4 + c for c in range(4)] + [(1 - zh) * 4 + x]
     far = [(1 - zh) * 4 + (x + d) % 4 for d in (2, 1, 3)]
@@ -276,33 +271,50 @@
     lax.fori_loop(5, 8, relay, 0)
     lax.fori_loop(5, 8, chip, 0)
     pl.semaphore_wait(group_sem, 7)
-    score(0, (1 - zh) * 4 + x, 0, range(8))
-
-    def other_tiles(i, _):
+
+    def far_tile(i):
+        return (1 - zh) * 4 + (x + i) % 4
+
+    def own_tile(i):
+        return zh * 4 + (x + 1 + i) % 4
+
+    def other_tile(i, previous):
         for head in range(4):
-            ahead = (x + i) % 4 if head < 3 else (x + i + 1) % 4
-            score((head + 1) % 4, (1 - zh) * 4 + ahead, (head + 1) % 2, range(8))
+            if previous is not None:
+                send_quarter(previous, head)
+            score((head + 1) % 4, far_tile(i if head < 3 else i + 1), (head + 1) % 2, range(8))
             slot = head % 2
             keep_head(head, sums(head, slot, range(8), tops[slot][0:1, :]))
-        send_tile((1 - zh) * 4 + (x + i) % 4)
-        return 0
-
-    lax.fori_loop(0, 4, other_tiles, 0)
-    score(0, zh * 4 + x, 0, far)
-
-    def second_part(i, _):
+        store_tile(far_tile(i))
+
+    def other_tiles(i, _):
+        other_tile(i, far_tile(i - 1))
+        return 0
+
+    def second_part(i, previous):
         for head in range(4):
-            ahead = (x + i) % 4 if head < 3 else (x + i + 1) % 4
-            score((head + 1) % 4, zh * 4 + ahead, (head + 1) % 2, far)
+            send_quarter(previous, head)
+            score((head + 1) % 4, own_tile(i if head < 3 else i + 1), (head + 1) % 2, far)
             slot = head % 2
-            before = held_top[(x + i) % 4, head, 0:1, :]
+            place = own_tile(i) - zh * 4
+            before = held_top[place, head, 0:1, :]
             top = jnp.maximum(tops[slot][0:1, :], before)
-            acc = held[(x + i) % 4, head] * jnp.exp2(before - top)
+            acc = held[place, head] * jnp.exp2(before - top)
             keep_head(head, acc + sums(head, slot, far, top))
-        send_tile(zh * 4 + (x + i) % 4)
-        return 0
-
-    lax.fori_loop(0, 4, second_part, 0)
+        store_tile(own_tile(i))
+
+    def second_parts(i, _):
+        second_part(i, own_tile(i - 1))
+        return 0
+
+    score(0, far_tile(0), 0, range(8))
+    other_tile(0, None)
+    lax.fori_loop(1, 4, other_tiles, 0)
+    score(0, own_tile(0), 0, far)
+    second_part(0, far_tile(3))
+    lax.fori_loop(1, 4, second_parts, 0)
+    for quarter in range(4):
+        send_quarter(own_tile(3), quarter, own=True)
 
     for load in loads:
         load.wait()

time: 101 us -> 103 us (1.020)
  Pallas kernels: 97.3 us -> 100 us
    pallas_call x1, Pallas kernels: 97.3 us -> 100 us  [shards(): pl.pallas_call(fused_kernel, name='blocks', out_shape=jax.ShapeDtypeStruc...]
where the time goes in v7:
time: 103 us
  Pallas kernels  100 us (97%)
  local copies, waits for them, and re-layouts  2.37 us (2%)
    pallas_call x1, Pallas kernels, shards(): pl.pallas_call(fused_kernel, name='blocks', out_shape=jax.ShapeDtypeStruc...  100 us
    transpose x1, local copies, waits for them, and re-layouts, shards(): parts.reshape(2, 8, 4, 8, D).transpose(2, 1, 0, 3, 4).reshape(4, 128, D)  2.37 us

profile of v7, /device:TPU:32, one launch (start us, length us, event | category | flops | bytes accessed | tf_op | source)
XLA Modules:
  0.0 102.5 jit_solution(11074365155317668141)
XLA Ops:
  0.0 100.1 %blocks.1 = bf16[2,8,32,1152]{3,2,1,0:T(8,128)(2,1)} custom-call(bf16[4,128,1152]{2,1,0:T(8,128)(2,1)} %tok_hbm.1, f32[3,1152]{1,0:T(4,128)} %mod_s.1, f32[3,1152]{1,0:T(4,128)} %mod_t.1, bf16[1152,3456]{1,0:T(8,128)(2,1)} %w_qkv_s.1, bf16[1152,1152]{1,0:T(8,128)(2,1)} %w_out_s.1, bf16[1152,3456]{1,0:T(8,128)(2,1)} %w_qkv_t.1, bf16[1152,1152]{1,0:T(8,128)(2,1)} %w_out_t.1), custom_call_target="tpu_custom_call" | custom-call | tf_op jit(solution)/shard_map/blocks/pallas_call | solution.py:405
  100.2 2.4 %copy.8 = bf16[4,8,2,8,1152]{4,3,2,1,0:T(8,128)(2,1)} copy(bf16[4,8,2,8,1152]{4,3,0,1,2:T(8,128)(2,1)} %bitcast.4) | data formatting | bytes 2359296 | tf_op jit(solution)/shard_map/transpose | solution.py:454

commit v8 on v6

--- a/solution.py
+++ b/solution.py
@@ -145,40 +145,47 @@
     norm(2 * (1 - zh))
     norm(2 * (1 - zh) + 1)
     pl.semaphore_wait(barrier, 22)
-    for j in range(2):
-        remote(hs.at[2 * (1 - zh) + j], zbuf.at[j], gather_send, z_sem.at[j], zdev).start()
+    parts = (pl.ds(0, 64), pl.ds(64, 64))
+    for r, part in enumerate(parts):
+        for j in range(2):
+            remote(hs.at[2 * (1 - zh) + j, part], zbuf.at[j, part], gather_send, z_sem.at[r, j], zdev).start()
     for d in range(1, 8):
         pl.semaphore_signal(group_sem, inc=1, device_id=((frame + d) % 8, patch), device_id_type=MESH)
     norm(2 * zh)
     norm(2 * zh + 1)
 
-    def along_x(chunk, source):
+    for r, part in enumerate(parts):
         for d in (2, 1, 3):
             xd = (x + d) % 4
-            remote(chunk(xd // 2), full.at[source], gather_send, full_sem.at[source], (frame, zh * 8 + xd * 2 + core)).start()
-        pltpu.make_async_copy(chunk(x // 2), full.at[source], full_sem.at[source]).start()
-
-    along_x(lambda j: hs.at[2 * zh + j], patch)
+            device = (frame, zh * 8 + xd * 2 + core)
+            src, dst = hs.at[2 * zh + xd // 2, part], full.at[patch, part]
+            remote(src, dst, gather_send, full_sem.at[r, patch], device).start()
+        src, dst = hs.at[2 * zh + x // 2, part], full.at[patch, part]
+        pltpu.make_async_copy(src, dst, full_sem.at[r, patch]).start()
     awide[...] = jnp.zeros_like(awide)
     for window in windows:
         window.wait()
     pack_weights(wbuf, packed, group)
 
-    def arrived(source):
-        pltpu.make_async_copy(full.at[source], full.at[source], full_sem.at[source]).wait()
+    def arrived(source, r):
+        spot = full.at[source, parts[r]]
+        pltpu.make_async_copy(spot, spot, full_sem.at[r, source]).wait()
 
     def chip_of(k):
         return ((zh + k // 4) % 2) * 4 + (x + 2 * (k % 4) - 3 * (k % 4 // 2)) % 4
 
     def relay(k, _):
         source = chip_of(k) * 2 + core
-        arrived(source)
-        remote(full.at[source], full.at[source], gather_send, full_sem.at[source], sibling).start()
+        for r in range(2):
+            arrived(source, r)
+            spot = full.at[source, parts[r]]
+            remote(spot, spot, gather_send, full_sem.at[r, source], sibling).start()
         return 0
 
     def chip(k, _):
         index = chip_of(k)
-        arrived(index * 2 + 1 - core)
+        for r in range(2):
+            arrived(index * 2 + 1 - core, r)
         h = full[pl.ds(index * 2, 2)].reshape(QT, D)
         project(h, packed, qk, vt, index)
         return 0
@@ -191,19 +198,21 @@
     pltpu.make_async_copy(tok.at[:, rows16(frame), :], tok_t.at[frame], tok_recv).start()
     relay(0, 0)
     chip(0, 0)
-    for j in range(2):
-        pltpu.make_async_copy(zbuf.at[j], zbuf.at[j], z_sem.at[j]).wait()
-        for n in range(2):
-            xd = 2 * j + n
-            src, dst = zbuf.at[j], full.at[zpatch]
-
-            @pl.when(xd != x)
-            def _():
-                remote(src, dst, gather_send, full_sem.at[zpatch], (frame, zh * 8 + xd * 2 + core)).start()
-
-            @pl.when(xd == x)
-            def _():
-                pltpu.make_async_copy(src, dst, full_sem.at[zpatch]).start()
+    for r, part in enumerate(parts):
+        for j in range(2):
+            src, dst = zbuf.at[j, part], full.at[zpatch, part]
+            pltpu.make_async_copy(src, src, z_sem.at[r, j]).wait()
+            for n in range(2):
+                xd = 2 * j + n
+
+                @pl.when(xd != x)
+                def _():
+                    device = (frame, zh * 8 + xd * 2 + core)
+                    remote(src, dst, gather_send, full_sem.at[r, zpatch], device).start()
+
+                @pl.when(xd == x)
+                def _():
+                    pltpu.make_async_copy(src, dst, full_sem.at[r, zpatch]).start()
 
     lax.fori_loop(1, 5, relay, 0)
     for d in (1, 3, 5, 7):
@@ -276,33 +285,39 @@
     lax.fori_loop(5, 8, relay, 0)
     lax.fori_loop(5, 8, chip, 0)
     pl.semaphore_wait(group_sem, 7)
-    score(0, (1 - zh) * 4 + x, 0, range(8))
-
-    def other_tiles(i, _):
+
+    def far_tile(i):
+        return (1 - zh) * 4 + (x + 2 * (i % 4) - 3 * (i % 4 // 2)) % 4
+
+    def own_tile(i):
+        return zh * 4 + (x + 1 + 2 * (i % 4) - 3 * (i % 4 // 2)) % 4
+
+    score(0, far_tile(0), 0, range(8))
+
+    def two_tiles(i, _):
         for head in range(4):
-            ahead = (x + i) % 4 if head < 3 else (x + i + 1) % 4
-            score((head + 1) % 4, (1 - zh) * 4 + ahead, (head + 1) % 2, range(8))
+            if head < 3:
+                score(head + 1, far_tile(i), (head + 1) % 2, range(8))
+            else:
+                score(0, own_tile(i), 0, far)
             slot = head % 2
             keep_head(head, sums(head, slot, range(8), tops[slot][0:1, :]))
-        send_tile((1 - zh) * 4 + (x + i) % 4)
-        return 0
-
-    lax.fori_loop(0, 4, other_tiles, 0)
-    score(0, zh * 4 + x, 0, far)
-
-    def second_part(i, _):
+        send_tile(far_tile(i))
         for head in range(4):
-            ahead = (x + i) % 4 if head < 3 else (x + i + 1) % 4
-            score((head + 1) % 4, zh * 4 + ahead, (head + 1) % 2, far)
+            if head < 3:
+                score(head + 1, own_tile(i), (head + 1) % 2, far)
+            else:
+                score(0, far_tile(i + 1), 0, range(8))
             slot = head % 2
-            before = held_top[(x + i) % 4, head, 0:1, :]
+            place = own_tile(i) - zh * 4
+            before = held_top[place, head, 0:1, :]
             top = jnp.maximum(tops[slot][0:1, :], before)
-            acc = held[(x + i) % 4, head] * jnp.exp2(before - top)
+            acc = held[place, head] * jnp.exp2(before - top)
             keep_head(head, acc + sums(head, slot, far, top))
-        send_tile(zh * 4 + (x + i) % 4)
-        return 0
-
-    lax.fori_loop(0, 4, second_part, 0)
+        send_tile(own_tile(i))
+        return 0
+
+    lax.fori_loop(0, 4, two_tiles, 0)
 
     for load in loads:
         load.wait()
@@ -426,8 +441,8 @@
             pltpu.VMEM((2, 8, 32, D), BF),
             dma,
             dma((6,)),
-            dma((2,)),
-            dma((16,)),
+            dma((2, 2)),
+            dma((2, 16)),
             dma,
             dma,
             dma,

time: 101 us -> 101 us (level); the launches traced: 99.7 us -> 101 us
  Pallas kernels: 97.3 us -> 98.6 us
    pallas_call x1, Pallas kernels: 97.3 us -> 98.6 us  [shards(): pl.pallas_call(fused_kernel, name='blocks', out_shape=jax.ShapeDtypeStruc...]
where the time goes in v8:
time: 101 us
  Pallas kernels  98.6 us (98%)
  local copies, waits for them, and re-layouts  2.37 us (2%)
    pallas_call x1, Pallas kernels, shards(): pl.pallas_call(fused_kernel, name='blocks', out_shape=jax.ShapeDtypeStruc...  98.6 us
    transpose x1, local copies, waits for them, and re-layouts, shards(): parts.reshape(2, 8, 4, 8, D).transpose(2, 1, 0, 3, 4).reshape(4, 128, D)  2.37 us

profile of v8, /device:TPU:32, one launch (start us, length us, event | category | flops | bytes accessed | tf_op | source)
XLA Modules:
  0.0 100.9 jit_solution(13527256100151050359)
XLA Ops:
  0.0 98.6 %blocks.1 = bf16[2,8,32,1152]{3,2,1,0:T(8,128)(2,1)} custom-call(bf16[4,128,1152]{2,1,0:T(8,128)(2,1)} %tok_hbm.1, f32[3,1152]{1,0:T(4,128)} %mod_s.1, f32[3,1152]{1,0:T(4,128)} %mod_t.1, bf16[1152,3456]{1,0:T(8,128)(2,1)} %w_qkv_s.1, bf16[1152,1152]{1,0:T(8,128)(2,1)} %w_out_s.1, bf16[1152,3456]{1,0:T(8,128)(2,1)} %w_qkv_t.1, bf16[1152,1152]{1,0:T(8,128)(2,1)} %w_out_t.1), custom_call_target="tpu_custom_call" | custom-call | tf_op jit(solution)/shard_map/blocks/pallas_call | solution.py:408
  98.6 2.4 %copy.8 = bf16[4,8,2,8,1152]{4,3,2,1,0:T(8,128)(2,1)} copy(bf16[4,8,2,8,1152]{4,3,0,1,2:T(8,128)(2,1)} %bitcast.4) | data formatting | bytes 2359296 | tf_op jit(solution)/shard_map/transpose | solution.py:457

commit v9 on v8

--- a/solution.py
+++ b/solution.py
@@ -113,11 +113,10 @@
     tok_hbm, mod_s, mod_t, w_qkv_s, w_out_s, w_qkv_t, w_out_t, out,
     tok, hs, zbuf, full, wbuf, packed, qk, vt, s0, s1, m0, m1, held, held_top, awide, att, att_t, tok_t, wo_s, wq, wo,
     flat, mid, hp, qkv, mixed_all, done,
-    tok_sem, w_sem, z_sem, full_sem, gather_send, tok_send, tok_recv, att_send, att_recv, home_send, home_recv, group_sem,
+    tok_sem, w_sem, z_sem, full_sem, gather_send, tok_send, tok_recv, att_send, att_recv, side_send, side_recv, home_send, home_recv, group_sem,
 ):
     frame, patch, zh, x, core = place()
     group = (x % 2) * 2 + core
-    at = frame * 4 + zh * 2 + x // 2
     zpatch = (1 - zh) * 8 + x * 2 + core
     sibling = (frame, patch + 1 - 2 * core)
     zdev = (frame, zpatch)
@@ -249,24 +248,24 @@
         awide[pl.ds(pl.multiple_of(32 * group + HD * head, 8), HD), :] = acc[:HD] / acc[HD : HD + 1]
 
     def send_tile(tile):
-        att[pl.ds(pl.multiple_of(tile * QT, QT), QT), :] = awide[...].T.astype(BF)
+        att[tile] = awide[...].T.astype(BF).reshape(2, 8, 16, WIN)
 
         def go(n, _):
-            f, p = (frame + n // 2) % 8, tile * 2 + n % 2
-            src, dst = att.at[rows16(p * 8 + f), :], att_t.at[group, at]
-            mine = (f == frame) & (p == patch)
+            f = (frame + n) % 8
+            src, dst = att.at[tile, :, f], att_t.at[:, core, x % 2, frame, zh, x // 2]
+            mine = (f == frame) & (tile == zh * 4 + x)
 
             @pl.when(jnp.logical_not(mine))
             def _():
-                remote(src, dst, att_send, att_recv, (f, p)).start()
+                remote(src, dst, att_send, att_recv.at[zh], (f, tile * 2 + core)).start()
 
             @pl.when(mine)
             def _():
-                pltpu.make_async_copy(src, dst, att_recv).start()
+                pltpu.make_async_copy(src, dst, att_recv.at[zh]).start()
 
             return 0
 
-        lax.fori_loop(0, 16, go, 0)
+        lax.fori_loop(0, 8, go, 0)
 
     near = [zh * 4 + c for c in range(4)] + [(1 - zh) * 4 + x]
     far = [(1 - zh) * 4 + (x + d) % 4 for d in (2, 1, 3)]
@@ -319,16 +318,25 @@
 
     lax.fori_loop(0, 4, two_tiles, 0)
 
+    for n in range(2):
+        z = (zh + 1 + n) % 2
+        came = att_t.at[:, core, :, :, z]
+        pltpu.make_async_copy(came, came, att_recv.at[z]).wait()
+        part = att_t.at[1 - core, core, :, :, z]
+        remote(part, part, side_send, side_recv.at[n], sibling).start()
+
     for load in loads:
         load.wait()
     pltpu.make_async_copy(tok_t, tok_t, tok_recv).wait()
-    pltpu.make_async_copy(att_t, att_t, att_recv).wait()
+    for n in range(2):
+        came = att_t.at[core, 1 - core, :, :, (zh + 1 + n) % 2]
+        pltpu.make_async_copy(came, came, side_recv.at[n]).wait()
     for tile in range(9):
         cols = slice(tile * 128, tile * 128 + 128)
         g, rest = min(tile // 2, 3), tile - 2 * min(tile // 2, 3)
-        part = att_t[g, :, :, rest * 128 : rest * 128 + 128].reshape(512, 128)
+        part = att_t[core, g % 2, g // 2, :, :, :, :, rest * 128 : rest * 128 + 128].reshape(512, 128)
         if rest == 0 and g > 0:
-            part = part + att_t[g - 1, :, :, 256:384].reshape(512, 128)
+            part = part + att_t[core, (g - 1) % 2, (g - 1) // 2, :, :, :, :, 256:384].reshape(512, 128)
         flat[:, cols] = part
 
     def finish_mid(i, _):
@@ -397,7 +405,11 @@
     lax.fori_loop(0, 2, eight_patches, 0)
     pltpu.make_async_copy(full, full, gather_send).wait()
     pltpu.make_async_copy(tok_t.at[pl.ds(0, 7)], tok_t.at[pl.ds(0, 7)], tok_send).wait()
-    pltpu.make_async_copy(att.at[pl.ds(0, 2032), :], att.at[pl.ds(0, 2032), :], att_send).wait()
+    pltpu.make_async_copy(att.at[pl.ds(0, 7)], att.at[pl.ds(0, 7)], att_send).wait()
+    last = att.at[7, :, pl.ds(0, 7)]
+    pltpu.make_async_copy(last, last, att_send).wait()
+    part = att_t.at[1 - core, core]
+    pltpu.make_async_copy(part, part, side_send).wait()
     for n in range(2):
         pltpu.make_async_copy(done.at[n, pl.ds(0, 7)], done.at[n, pl.ds(0, 7)], home_send).wait()
     pltpu.make_async_copy(out, out, home_recv).wait()
@@ -427,8 +439,8 @@
             pltpu.VMEM((4, 4, 80, QT), F32),
             pltpu.VMEM((4, 4, 8, QT), F32),
             pltpu.VMEM((WIN, QT), F32),
-            pltpu.VMEM((ROWS, WIN), BF),
-            pltpu.VMEM((4, 32, 16, WIN), BF),
+            pltpu.VMEM((8, 2, 8, 16, WIN), BF),
+            pltpu.VMEM((2, 2, 2, 8, 2, 2, 16, WIN), BF),
             pltpu.VMEM((8, 4, 16, D), BF),
             pltpu.VMEM((D, D), BF),
             pltpu.VMEM((D, 3 * D), BF),
@@ -447,7 +459,9 @@
             dma,
             dma,
             dma,
-            dma,
+            dma((2,)),
+            dma,
+            dma((2,)),
             dma,
             dma,
             pltpu.SemaphoreType.REGULAR,

time: 101 us -> 103 us (1.020)
  Pallas kernels: 98.6 us -> 100 us
    pallas_call x1, Pallas kernels: 98.6 us -> 100 us  [shards(): pl.pallas_call(fused_kernel, name='blocks', out_shape=jax.ShapeDtypeStruc...]
where the time goes in v9:
time: 103 us
  Pallas kernels  100 us (97%)
  local copies, waits for them, and re-layouts  2.37 us (2%)
    pallas_call x1, Pallas kernels, shards(): pl.pallas_call(fused_kernel, name='blocks', out_shape=jax.ShapeDtypeStruc...  100 us
    transpose x1, local copies, waits for them, and re-layouts, shards(): parts.reshape(2, 8, 4, 8, D).transpose(2, 1, 0, 3, 4).reshape(4, 128, D)  2.37 us

profile of v9, /device:TPU:32, one launch (start us, length us, event | category | flops | bytes accessed | tf_op | source)
XLA Modules:
  0.0 102.6 jit_solution(9851391923309896857)
XLA Ops:
  0.0 100.2 %blocks.1 = bf16[2,8,32,1152]{3,2,1,0:T(8,128)(2,1)} custom-call(bf16[4,128,1152]{2,1,0:T(8,128)(2,1)} %tok_hbm.1, f32[3,1152]{1,0:T(4,128)} %mod_s.1, f32[3,1152]{1,0:T(4,128)} %mod_t.1, bf16[1152,3456]{1,0:T(8,128)(2,1)} %w_qkv_s.1, bf16[1152,1152]{1,0:T(8,128)(2,1)} %w_out_s.1, bf16[1152,3456]{1,0:T(8,128)(2,1)} %w_qkv_t.1, bf16[1152,1152]{1,0:T(8,128)(2,1)} %w_out_t.1), custom_call_target="tpu_custom_call" | custom-call | tf_op jit(solution)/shard_map/blocks/pallas_call | solution.py:420
  100.2 2.4 %copy.8 = bf16[4,8,2,8,1152]{4,3,2,1,0:T(8,128)(2,1)} copy(bf16[4,8,2,8,1152]{4,3,0,1,2:T(8,128)(2,1)} %bitcast.4) | data formatting | bytes 2359296 | tf_op jit(solution)/shard_map/transpose | solution.py:471

commit v10 on v8

--- a/solution.py
+++ b/solution.py
@@ -117,7 +117,7 @@
 ):
     frame, patch, zh, x, core = place()
     group = (x % 2) * 2 + core
-    at = frame * 4 + zh * 2 + x // 2
+    at = zh * 2 + x // 2
     zpatch = (1 - zh) * 8 + x * 2 + core
     sibling = (frame, patch + 1 - 2 * core)
     zdev = (frame, zpatch)
@@ -253,16 +253,16 @@
 
         def go(n, _):
             f, p = (frame + n // 2) % 8, tile * 2 + n % 2
-            src, dst = att.at[rows16(p * 8 + f), :], att_t.at[group, at]
+            src, dst = att.at[rows16(p * 8 + f), :], att_t.at[group, frame, at]
             mine = (f == frame) & (p == patch)
 
             @pl.when(jnp.logical_not(mine))
             def _():
-                remote(src, dst, att_send, att_recv, (f, p)).start()
+                remote(src, dst, att_send, att_recv.at[zh], (f, p)).start()
 
             @pl.when(mine)
             def _():
-                pltpu.make_async_copy(src, dst, att_recv).start()
+                pltpu.make_async_copy(src, dst, att_recv.at[zh]).start()
 
             return 0
 
@@ -292,29 +292,29 @@
     def own_tile(i):
         return zh * 4 + (x + 1 + 2 * (i % 4) - 3 * (i % 4 // 2)) % 4
 
-    score(0, far_tile(0), 0, range(8))
+    score(0, own_tile(0), 0, far)
 
     def two_tiles(i, _):
+        for head in range(4):
+            if head < 3:
+                score(head + 1, own_tile(i), (head + 1) % 2, far)
+            else:
+                score(0, far_tile(i), 0, range(8))
+            slot = head % 2
+            spot = own_tile(i) - zh * 4
+            before = held_top[spot, head, 0:1, :]
+            top = jnp.maximum(tops[slot][0:1, :], before)
+            acc = held[spot, head] * jnp.exp2(before - top)
+            keep_head(head, acc + sums(head, slot, far, top))
+        send_tile(own_tile(i))
         for head in range(4):
             if head < 3:
                 score(head + 1, far_tile(i), (head + 1) % 2, range(8))
             else:
-                score(0, own_tile(i), 0, far)
+                score(0, own_tile(i + 1), 0, far)
             slot = head % 2
             keep_head(head, sums(head, slot, range(8), tops[slot][0:1, :]))
         send_tile(far_tile(i))
-        for head in range(4):
-            if head < 3:
-                score(head + 1, own_tile(i), (head + 1) % 2, far)
-            else:
-                score(0, far_tile(i + 1), 0, range(8))
-            slot = head % 2
-            place = own_tile(i) - zh * 4
-            before = held_top[place, head, 0:1, :]
-            top = jnp.maximum(tops[slot][0:1, :], before)
-            acc = held[place, head] * jnp.exp2(before - top)
-            keep_head(head, acc + sums(head, slot, far, top))
-        send_tile(own_tile(i))
         return 0
 
     lax.fori_loop(0, 4, two_tiles, 0)
@@ -322,26 +322,28 @@
     for load in loads:
         load.wait()
     pltpu.make_async_copy(tok_t, tok_t, tok_recv).wait()
-    pltpu.make_async_copy(att_t, att_t, att_recv).wait()
-    for tile in range(9):
-        cols = slice(tile * 128, tile * 128 + 128)
-        g, rest = min(tile // 2, 3), tile - 2 * min(tile // 2, 3)
-        part = att_t[g, :, :, rest * 128 : rest * 128 + 128].reshape(512, 128)
-        if rest == 0 and g > 0:
-            part = part + att_t[g - 1, :, :, 256:384].reshape(512, 128)
-        flat[:, cols] = part
-
-    def finish_mid(i, _):
-        rows = pl.ds(pl.multiple_of(i * 256, 256), 256)
-        proj = jnp.dot(flat[rows, :], wo_s[...], preferred_element_type=F32)
-        values = tok_t[pl.ds(i * 4, 4)].reshape(256, D).astype(F32)
-        values = (values + mod_s[2:3, :] * proj).astype(BF)
-        mid[pl.ds(i * 16, 16)] = values.astype(F32).reshape(16, 16, D)
-        flat[rows, :] = modulate(values.astype(F32), mod_t)
+
+    def finish_mid(n, _):
+        z = (zh + n) % 2
+        came = att_t.at[:, :, pl.ds(2 * z, 2)]
+        pltpu.make_async_copy(came, came, att_recv.at[z]).wait()
+        frames = pl.ds(2 * z, 2)
+        tiles = []
+        for tile in range(9):
+            g, rest = min(tile // 2, 3), tile - 2 * min(tile // 2, 3)
+            part = att_t[g, :, frames, :, rest * 128 : rest * 128 + 128].reshape(256, 128)
+            if rest == 0 and g > 0:
+                part = part + att_t[g - 1, :, frames, :, 256:384].reshape(256, 128)
+            tiles.append(part)
+        proj = jnp.dot(jnp.concatenate(tiles, axis=1), wo_s[...], preferred_element_type=F32)
+        values = tok_t[:, frames].reshape(256, D).astype(F32)
+        values = (values + mod_s[2:3, :] * proj).astype(BF).astype(F32)
+        mid[:, frames] = values.reshape(8, 2, 16, D)
+        flat[:, frames] = modulate(values, mod_t).reshape(8, 2, 16, D)
         return 0
 
     lax.fori_loop(0, 2, finish_mid, 0)
-    hp[...] = jnp.dot(to_patches(), flat[...], preferred_element_type=F32).astype(BF)
+    hp[...] = jnp.dot(to_patches(), flat[...].reshape(512, D), preferred_element_type=F32).astype(BF)
 
     row = lax.broadcasted_iota(jnp.int32, (128, 128), 0)
     col = lax.broadcasted_iota(jnp.int32, (128, 128), 1)
@@ -381,7 +383,7 @@
         lax.fori_loop(0, 2, four_patches, 0)
         ordered = jnp.dot(to_frames(), mixed_all[...], preferred_element_type=F32).astype(BF)
         proj = jnp.dot(ordered, wo[...], preferred_element_type=F32)
-        values = mid[:, pl.ds(pl.multiple_of(n * 8, 8), 8), :].reshape(256, D)
+        values = mid[:, :, pl.ds(pl.multiple_of(n * 8, 8), 8), :].reshape(256, D)
         values = (values + mod_t[2:3, :] * proj).astype(BF)
         done[n] = values.reshape(8, 32, D)
 
@@ -428,13 +430,13 @@
             pltpu.VMEM((4, 4, 8, QT), F32),
             pltpu.VMEM((WIN, QT), F32),
             pltpu.VMEM((ROWS, WIN), BF),
-            pltpu.VMEM((4, 32, 16, WIN), BF),
+            pltpu.VMEM((4, 8, 4, 16, WIN), BF),
             pltpu.VMEM((8, 4, 16, D), BF),
             pltpu.VMEM((D, D), BF),
             pltpu.VMEM((D, 3 * D), BF),
             pltpu.VMEM((D, D), BF),
-            pltpu.VMEM((512, D), BF),
-            pltpu.VMEM((32, 16, D), F32),
+            pltpu.VMEM((8, 4, 16, D), BF),
+            pltpu.VMEM((8, 4, 16, D), F32),
             pltpu.VMEM((512, D), BF),
             pltpu.VMEM((256, 3 * D), BF),
             pltpu.VMEM((256, D), BF),
@@ -447,7 +449,7 @@
             dma,
             dma,
             dma,
-            dma,
+            dma((2,)),
             dma,
             dma,
             pltpu.SemaphoreType.REGULAR,

time: 101 us -> 99.9 us (0.989)
  Pallas kernels: 98.6 us -> 97.3 us
    pallas_call x1, Pallas kernels: 98.6 us -> 97.3 us  [shards(): pl.pallas_call(fused_kernel, name='blocks', out_shape=jax.ShapeDtypeStruc...]
where the time goes in v10:
time: 99.9 us; the launch traced here: 99.7 us
  Pallas kernels  97.3 us (97%)
  local copies, waits for them, and re-layouts  2.37 us (2%)
    pallas_call x1, Pallas kernels, shards(): pl.pallas_call(fused_kernel, name='blocks', out_shape=jax.ShapeDtypeStruc...  97.3 us
    transpose x1, local copies, waits for them, and re-layouts, shards(): parts.reshape(2, 8, 4, 8, D).transpose(2, 1, 0, 3, 4).reshape(4, 128, D)  2.37 us

profile of v10, /device:TPU:32, one launch (start us, length us, event | category | flops | bytes accessed | tf_op | source)
XLA Modules:
  0.0 99.7 jit_solution(14457000333225611050)
XLA Ops:
  0.0 97.3 %blocks.1 = bf16[2,8,32,1152]{3,2,1,0:T(8,128)(2,1)} custom-call(bf16[4,128,1152]{2,1,0:T(8,128)(2,1)} %tok_hbm.1, f32[3,1152]{1,0:T(4,128)} %mod_s.1, f32[3,1152]{1,0:T(4,128)} %mod_t.1, bf16[1152,3456]{1,0:T(8,128)(2,1)} %w_qkv_s.1, bf16[1152,1152]{1,0:T(8,128)(2,1)} %w_out_s.1, bf16[1152,3456]{1,0:T(8,128)(2,1)} %w_qkv_t.1, bf16[1152,1152]{1,0:T(8,128)(2,1)} %w_out_t.1), custom_call_target="tpu_custom_call" | custom-call | tf_op jit(solution)/shard_map/blocks/pallas_call | solution.py:410
  97.3 2.4 %copy.8 = bf16[4,8,2,8,1152]{4,3,2,1,0:T(8,128)(2,1)} copy(bf16[4,8,2,8,1152]{4,3,0,1,2:T(8,128)(2,1)} %bitcast.4) | data formatting | bytes 2359296 | tf_op jit(solution)/shard_map/transpose | solution.py:459

commit v11 on v10

--- a/solution.py
+++ b/solution.py
@@ -144,6 +144,8 @@
     load_tok.wait()
     norm(2 * (1 - zh))
     norm(2 * (1 - zh) + 1)
+    norm(2 * zh)
+    norm(2 * zh + 1)
     pl.semaphore_wait(barrier, 22)
     parts = (pl.ds(0, 64), pl.ds(64, 64))
     for r, part in enumerate(parts):
@@ -151,8 +153,6 @@
             remote(hs.at[2 * (1 - zh) + j, part], zbuf.at[j, part], gather_send, z_sem.at[r, j], zdev).start()
     for d in range(1, 8):
         pl.semaphore_signal(group_sem, inc=1, device_id=((frame + d) % 8, patch), device_id_type=MESH)
-    norm(2 * zh)
-    norm(2 * zh + 1)
 
     for r, part in enumerate(parts):
         for d in (2, 1, 3):
@@ -382,18 +382,21 @@
             qkv[:, cols] = acc.astype(BF)
         lax.fori_loop(0, 2, four_patches, 0)
         ordered = jnp.dot(to_frames(), mixed_all[...], preferred_element_type=F32).astype(BF)
-        proj = jnp.dot(ordered, wo[...], preferred_element_type=F32)
         values = mid[:, :, pl.ds(pl.multiple_of(n * 8, 8), 8), :].reshape(256, D)
-        values = (values + mod_t[2:3, :] * proj).astype(BF)
-        done[n] = values.reshape(8, 32, D)
-
-        def go(d, _):
-            f = (frame + d) % 8
-            remote(done.at[n, f], out.at[n, frame], home_send, home_recv, (f, patch)).start()
-            return 0
-
-        lax.fori_loop(1, 8, go, 0)
-        pltpu.make_async_copy(done.at[n, frame], out.at[n, frame], home_recv).start()
+        for cols in (slice(0, 512), slice(512, 1152)):
+            proj = jnp.dot(ordered, wo[:, cols], preferred_element_type=F32)
+            block = (values[:, cols] + mod_t[2:3, cols] * proj).astype(BF)
+            done[n, :, :, cols] = block.reshape(8, 32, cols.stop - cols.start)
+
+            def go(d, _):
+                f = (frame + d) % 8
+                src, dst = done.at[n, f, :, cols], out.at[n, frame, :, cols]
+                remote(src, dst, home_send, home_recv, (f, patch)).start()
+                return 0
+
+            lax.fori_loop(1, 8, go, 0)
+            src, dst = done.at[n, frame, :, cols], out.at[n, frame, :, cols]
+            pltpu.make_async_copy(src, dst, home_recv).start()
         return 0
 
     lax.fori_loop(0, 2, eight_patches, 0)
@@ -403,6 +406,12 @@
     for n in range(2):
         pltpu.make_async_copy(done.at[n, pl.ds(0, 7)], done.at[n, pl.ds(0, 7)], home_send).wait()
     pltpu.make_async_copy(out, out, home_recv).wait()
+
+
+def order_kernel(parts, out):
+    for f in range(parts.shape[1]):
+        first, second = (parts[n, f].astype(F32).reshape(4, 8, D) for n in range(2))
+        out[:, f * 16 : f * 16 + 16, :] = jnp.concatenate([first, second], axis=1).astype(BF)
 
 
 def shards(tokens, w_qkv_s, w_out_s, mod_s, w_qkv_t, w_out_t, mod_t):
@@ -456,7 +465,16 @@
         ],
         compiler_params=params(1),
     )(tokens, mod_s, mod_t, w_qkv_s, w_out_s, w_qkv_t, w_out_t)
-    return parts.reshape(2, 8, 4, 8, D).transpose(2, 1, 0, 3, 4).reshape(4, 128, D)
+    steps = 2
+    return pl.pallas_call(
+        order_kernel,
+        name="order",
+        grid=(steps,),
+        out_shape=jax.ShapeDtypeStruct((4, 128, D), BF),
+        in_specs=[pl.BlockSpec((2, 8 // steps, 32, D), lambda i: (0, i, 0, 0))],
+        out_specs=pl.BlockSpec((4, 128 // steps, D), lambda i: (0, i, 0)),
+        compiler_params=params(),
+    )(parts)
 
 
 def solution(mesh):

time: 99.9 us -> 99.6 us (level)
  local copies, waits for them, and re-layouts: 2.37 us -> 0 us
  Pallas kernels: 97.3 us -> 99.4 us
    transpose x1 -> x0, local copies, waits for them, and re-layouts: 2.37 us -> none  [shards(): parts.reshape(2, 8, 4, 8, D).transpose(2, 1, 0, 3, 4).reshape(4, 128, D)]
    pallas_call x0 -> x1, Pallas kernels: none -> 2.13 us  [shards(): pl.pallas_call(order_kernel, name='order', grid=(steps,), out_shape=jax.S...]
where the time goes in v11:
time: 99.6 us; the launch traced here: 99.4 us
  Pallas kernels  99.4 us (100%)
    pallas_call x1, Pallas kernels, shards(): pl.pallas_call(fused_kernel, name='blocks', out_shape=jax.ShapeDtypeStruc...  97.2 us
    pallas_call x1, Pallas kernels, shards(): pl.pallas_call(order_kernel, name='order', grid=(steps,), out_shape=jax.S...  2.13 us

profile of v11, /device:TPU:32, one launch (start us, length us, event | category | flops | bytes accessed | tf_op | source)
XLA Modules:
  0.0 99.4 jit_solution(4322716143495766348)
XLA Ops:
  0.0 97.2 %blocks.1.parts = bf16[2,8,32,1152]{3,2,1,0:T(8,128)(2,1)} custom-call(bf16[4,128,1152]{2,1,0:T(8,128)(2,1)} %tok_hbm.1, f32[3,1152]{1,0:T(4,128)} %mod_s.1, f32[3,1152]{1,0:T(4,128)} %mod_t.1, bf16[1152,3456]{1,0:T(8,128)(2,1)} %w_qkv_s.1, bf16[1152,1152]{1,0:T(8,128)(2,1)} %w_out_s.1, bf16[1152,3456]{1,0:T(8,128)(2,1)} %w_qkv_t.1, bf16[1152,1152]{1,0:T(8,128)(2,1)} %w_out_t.1), custom_call_target="tpu_custom_call" | custom-call | tf_op jit(solution)/shard_map/blocks/pallas_call | solution.py:419
  97.3 2.1 %order.1 = bf16[4,128,1152]{2,1,0:T(8,128)(2,1)} custom-call(bf16[2,8,32,1152]{3,2,1,0:T(8,128)(2,1)} %blocks.1.parts), custom_call_target="tpu_custom_call" | custom-call | tf_op jit(solution)/shard_map/order/pallas_call | solution.py:469
